TPU v7x, 128 devices: a whole 4x4x4 slice. The times are simulated.
128 devices in a mesh: frame: 16 (over x, y), tile: 8 (over z, core).
Axes of the slice: x: 4, y: 4, z: 4, core: 2. Of those that a mesh axis runs over, the one named last changes fastest.
Arguments:
- grid: bfloat16 [64, 32, 32, 2048], P(None, 'frame', None, 'tile'), may hold values from -6 to 6
- conv_weight: bfloat16 [9, 64, 8], replicated, may hold values from -0.75 to 0.75
- conv_bias: float32 [64], replicated, may hold values from -3 to 3
- depth_kernel: float32 [4, 3, 64], replicated, may hold values from -3 to 3
- point_weight: bfloat16 [4, 64, 64], replicated, may hold values from -0.75 to 0.75
- occupied: int32 [8, 32], P('tile'), may hold values from 0 to 63, as said below
- counts: int32 [8], P('tile'), may hold values from 10 to 32, as said below
Outputs:
- features: bfloat16 [64, 32, 32, 2048], P(None, 'frame', None, 'tile')
Inputs may be any that keep to these rules, and one draw needn't show every extreme that they name: Each row holds 32 distinct block numbers of its tile; its first counts[t] entries are the occupied blocks, the rest are unoccupied blocks used as padding. `counts`: some tile's list is fully occupied, and some tile has exactly the fewest occupied entries.
All inputs are finite; a program needn't handle non-finite values.
Results may differ from a plain program's by a relative error of at most 0.0051.
Values may be sent and summed in bfloat16 or wider, within the bound.
A program may use at most 128 MiB of HBM per device.

v0:
```python
import jax
import jax.numpy as jnp
from jax import lax
from jax.sharding import PartitionSpec as P

GROUP = 8


def with_halo(cells, sides, width):
    for axis, dim in sides:
        count = lax.axis_size(axis)
        ends = count - 1
        head = lax.slice_in_dim(cells, 0, width, axis=dim)
        tail = lax.slice_in_dim(cells, cells.shape[dim] - width, cells.shape[dim], axis=dim)
        cells = jnp.concatenate(
            [
                lax.ppermute(tail, axis, [(i, (i + 1) % count) for i in range(ends)]),
                cells,
                lax.ppermute(head, axis, [((i + 1) % count, i) for i in range(ends)]),
            ],
            axis=dim,
        )
    return cells


def shifted(series, amount):
    if amount == 0:
        return series
    frames = series.shape[1]
    leading = jnp.zeros_like(series[:, :amount])
    return jnp.concatenate([leading, series[:, : frames - amount]], axis=1)


def temporal(blocks, depth_kernel, point_weight):
    current = blocks.astype(jnp.float32)
    for layer_idx in range(depth_kernel.shape[0]):
        spacing = 2**layer_idx
        blended = jnp.zeros_like(current)
        for offset in range(depth_kernel.shape[1]):
            blended = blended + depth_kernel[layer_idx, offset][:, None, None, None] * shifted(
                current, offset * spacing
            )
        squashed = jax.nn.silu(blended).astype(jnp.bfloat16)
        current = current + jnp.einsum(
            "oc,cfsn->ofsn", point_weight[layer_idx], squashed, preferred_element_type=jnp.float32
        )
    return current.astype(jnp.bfloat16)


def spatial(padded, center, conv_weight, conv_bias):
    channels, frames, height, columns = center.shape
    group_count = channels // GROUP
    grouped = padded.reshape(group_count, GROUP, frames, height + 2, columns + 2)
    summed = jnp.zeros((group_count, GROUP, frames, height, columns), jnp.float32)
    for tap_row in range(3):
        for tap_col in range(3):
            window = grouped[:, :, :, tap_row : tap_row + height, tap_col : tap_col + columns]
            kernel = conv_weight[tap_row * 3 + tap_col].reshape(group_count, GROUP, GROUP)
            summed = summed + jnp.einsum(
                "goi,gifrw->gofrw", kernel, window, preferred_element_type=jnp.float32
            )
    activation = summed.reshape(channels, frames, height, columns) + conv_bias[:, None, None, None]
    return (center.astype(jnp.float32) + jax.nn.silu(activation)).astype(jnp.bfloat16)


def on_device(grid, conv_weight, conv_bias, depth_kernel, point_weight, occupied, counts):
    widened = with_halo(grid, (("tile", 3),), 1)
    padded = jnp.pad(widened, ((0, 0), (0, 0), (1, 1), (0, 0)))
    hidden = spatial(padded, grid, conv_weight, conv_bias)
    channels, frames, height, columns = grid.shape
    blocks = hidden.reshape(channels, frames, height * (columns // 128), 128)
    block_ids = occupied[0]
    slot_count = block_ids.shape[0]
    live_slots = jnp.arange(slot_count, dtype=jnp.int32) < counts[0]
    picked = jnp.take(blocks, block_ids, axis=2)
    updated = lax.all_to_all(
        temporal(
            lax.all_to_all(picked, "frame", split_axis=2, concat_axis=1, tiled=True),
            depth_kernel,
            point_weight,
        ),
        "frame",
        split_axis=1,
        concat_axis=2,
        tiled=True,
    )
    chosen = jnp.where(live_slots[None, None, :, None], updated, picked)
    blocks = blocks.at[:, :, block_ids].set(chosen)
    return blocks.reshape(channels, frames, height, columns)


def solution(mesh):
    placed = (P(None, "frame", None, "tile"), P(), P(), P(), P(), P("tile", None), P("tile"))
    return jax.shard_map(
        on_device,
        mesh=mesh,
        in_specs=placed,
        out_specs=P(None, "frame", None, "tile"),
        check_vma=False,
    )
```

profile of v0, /device:TPU:0, one launch (start us, length us, event | category | flops | bytes accessed | tf_op | source)
XLA Modules:
  0.0 146.3 jit_solution(1894894144951527090)
XLA Ops:
  0.0 3.0 %fusion.64 = (bf16[64,2,32,1]{3,2,1,0:T(8,128)(2,1)}, bf16[64,2,32,1]{3,2,1,0:T(8,128)(2,1)S(1)}) fusion(bf16[64,2,32,256]{3,2,1,0:T(8,128)(2,1)} %param.7), kind=kLoop, calls=%fused_computation.98 | loop fusion | bytes 32768 | tf_op jit(solution)/shard_map/slice | solution.py:14
  3.0 2.5 %copy.115 = bf16[64,2,32,1]{0,2,3,1:T(8,128)(2,1)S(1)} copy(bf16[64,2,32,1]{3,2,1,0:T(8,128)(2,1)} %get-tuple-element.14) | data formatting | bytes 16384
  5.6 1.3 collective-permute-start
  6.8 1.2 copy.116
  8.1 1.3 collective-permute-start.1
  9.5 2.5 %copy.76 = bf16[64,2,32,256]{3,0,2,1:T(8,128)(2,1)} copy(bf16[64,2,32,256]{3,2,1,0:T(8,128)(2,1)S(1)} %copy-done) | data formatting | bytes 4194304 | tf_op args[0]
  12.9 0.5 copy.75
  13.4 1.5 %copy.77 = bf16[64,2,32,1]{3,0,2,1:T(8,128)(2,1)} copy(bf16[64,2,32,1]{0,2,3,1:T(8,128)(2,1)S(1)} %collective-permute-done.1) | data formatting | bytes 16384 | tf_op jit(solution)/shard_map/ppermute | solution.py:19
  14.9 3.6 %fusion.6 = bf16[8,8,2,34,258]{4,1,0,3,2:T(8,128)(2,1)S(1)} fusion(bf16[64,2,32,1]{3,0,2,1:T(8,128)(2,1)} %copy.77, bf16[64,2,32,256]{3,0,2,1:T(8,128)(2,1)} %copy.76, bf16[64,2,32,1]{3,0,2,1:T(8,128)(2,1)S(1)} %copy.75), kind=kLoop, calls=%fused_computation.13 | loop fusion | flops 13473792 | bytes 4359168 | tf_op jit(solution)/shard_map/reshape | solution.py:53
  18.5 7.9 %fusion.63 = (bf16[8,8,2,32,256]{4,1,0,3,2:T(8,128)(2,1)S(1)}, bf16[8,8,2,32,256]{4,1,0,3,2:T(8,128)(2,1)}, bf16[8,8,2,32,256]{4,1,0,3,2:T(8,128)(2,1)}, bf16[8,...) fusion(bf16[8,8,2,34,258]{4,1,0,3,2:T(8,128)(2,1)S(1)} %fusion.6), kind=kLoop, calls=%fused_computation.97 | loop fusion | bytes 37748736 | tf_op jit(solution)/shard_map/slice | solution.py:57
  26.5 2.4 %fusion.10 = f32[8,2,32,256,8]{3,4,2,1,0:T(8,128)S(1)} fusion(bf16[8,8,2,32,256]{4,1,0,3,2:T(8,128)(2,1)} %get-tuple-element.7, bf16[1,64,8]{2,1,0:T(8,128)(2,1)S(1)} %copy.91), kind=kOutput, calls=%fused_computation.17 | convolution fusion | flops 16777216 | bytes 6292480 | tf_op jit(solution)/shard_map/goi,gifrw->gofrw/dot_general | solution.py:59
  28.9 2.6 %fusion.12 = f32[8,2,32,256,8]{3,4,2,1,0:T(8,128)} fusion(bf16[8,8,2,32,256]{4,1,0,3,2:T(8,128)(2,1)S(1)} %copy-done.7, bf16[1,64,8]{2,1,0:T(8,128)(2,1)S(1)} %copy.89), kind=kOutput, calls=%fused_computation.19 | convolution fusion | flops 16777216 | bytes 6292480 | tf_op jit(solution)/shard_map/goi,gifrw->gofrw/dot_general | solution.py:59
  31.6 2.7 %fusion.14 = f32[8,2,32,256,8]{3,4,2,1,0:T(8,128)} fusion(bf16[8,8,2,32,256]{4,1,0,3,2:T(8,128)(2,1)S(1)} %copy-done.6, bf16[1,64,8]{2,1,0:T(8,128)(2,1)S(1)} %copy.87), kind=kOutput, calls=%fused_computation.21 | convolution fusion | flops 16777216 | bytes 6292480 | tf_op jit(solution)/shard_map/goi,gifrw->gofrw/dot_general | solution.py:59
  34.2 2.7 %fusion.16 = f32[8,2,32,256,8]{3,4,2,1,0:T(8,128)} fusion(bf16[8,8,2,32,256]{4,1,0,3,2:T(8,128)(2,1)S(1)} %copy-done.5, bf16[1,64,8]{2,1,0:T(8,128)(2,1)S(1)} %copy.85), kind=kOutput, calls=%fused_computation.23 | convolution fusion | flops 16777216 | bytes 6292480 | tf_op jit(solution)/shard_map/goi,gifrw->gofrw/dot_general | solution.py:59
  36.9 2.6 %fusion.18 = f32[8,2,32,256,8]{3,4,2,1,0:T(8,128)} fusion(bf16[8,8,2,32,256]{4,1,0,3,2:T(8,128)(2,1)S(1)} %copy-done.4, bf16[1,64,8]{2,1,0:T(8,128)(2,1)S(1)} %copy.83), kind=kOutput, calls=%fused_computation.25 | convolution fusion | flops 16777216 | bytes 6292480 | tf_op jit(solution)/shard_map/goi,gifrw->gofrw/dot_general | solution.py:59
  39.6 2.6 %fusion.20 = f32[8,2,32,256,8]{3,4,2,1,0:T(8,128)} fusion(bf16[8,8,2,32,256]{4,1,0,3,2:T(8,128)(2,1)S(1)} %copy-done.3, bf16[1,64,8]{2,1,0:T(8,128)(2,1)S(1)} %copy.81), kind=kOutput, calls=%fused_computation.27 | convolution fusion | flops 16777216 | bytes 6292480 | tf_op jit(solution)/shard_map/goi,gifrw->gofrw/dot_general | solution.py:59
  42.2 2.7 %fusion.22 = f32[8,2,32,256,8]{3,4,2,1,0:T(8,128)} fusion(bf16[8,8,2,32,256]{4,1,0,3,2:T(8,128)(2,1)S(1)} %copy-done.2, bf16[1,64,8]{2,1,0:T(8,128)(2,1)S(1)} %copy.79), kind=kOutput, calls=%fused_computation.29 | convolution fusion | flops 16777216 | bytes 6292480 | tf_op jit(solution)/shard_map/goi,gifrw->gofrw/dot_general | solution.py:59
  44.9 2.7 %fusion.8 = f32[8,2,32,256,8]{3,4,2,1,0:T(8,128)} fusion(bf16[8,8,2,32,256]{4,1,0,3,2:T(8,128)(2,1)S(1)} %copy-done.1, bf16[1,64,8]{2,1,0:T(8,128)(2,1)S(1)} %copy.93), kind=kOutput, calls=%fused_computation.15 | convolution fusion | flops 16777216 | bytes 6292480 | tf_op jit(solution)/shard_map/goi,gifrw->gofrw/dot_general | solution.py:59
  47.5 12.9 %add_bitcast_fusion = f32[8,8,2,32,256]{4,1,3,2,0:T(8,128)} fusion(f32[8,2,32,256,8]{3,4,2,1,0:T(8,128)} %fusion.8, f32[8,2,32,256,8]{3,4,2,1,0:T(8,128)S(1)} %fusion.10, f32[8,2,32,256,8]{3,4,2,1,0:T(8,128)} %fusion.12, f32[8,2,32,256,8]{3,4,2,1,0:T(8,128)} %fusion.14, f32[8,2,32,256,8]{3,4,2,1,0:T(8,128)} %fusion.16, f32[8,2,32,256,8]{3,4,2,1,0:T(8,128)} %fusion.18, ...), kind=kOutput, calls=%fused_computation.6 | convolution fusion | flops 25165824 | bytes 39846912 | tf_op jit(solution)/shard_map/goi,gifrw->gofrw/dot_general | solution.py:59
  60.4 3.5 %copy.96 = f32[8,8,2,32,256]{4,3,2,1,0:T(8,128)S(1)} copy(f32[8,8,2,32,256]{4,1,3,2,0:T(8,128)} %add_bitcast_fusion) | data formatting | bytes 8388608 | tf_op jit(solution)/shard_map/add | solution.py:59
  63.9 3.3 %add_convert_fusion = bf16[64,2,32,256]{3,2,1,0:T(8,128)(2,1)} fusion(f32[8,8,2,32,256]{4,3,2,1,0:T(8,128)S(1)} %copy.96, bf16[64,2,32,256]{3,2,1,0:T(8,128)(2,1)S(1)} %copy-done, f32[64]{0:T(128)S(1)} %copy-done.10), kind=kLoop, calls=%fused_computation.7 | loop fusion | flops 8388608 | bytes 8388864 | tf_op jit(solution)/shard_map/convert_element_type | solution.py:63
  67.2 4.1 %reshape.69 = bf16[64,2,64,128]{3,2,1,0:T(8,128)(2,1)} reshape(bf16[64,2,32,256]{3,2,1,0:T(8,128)(2,1)} %add_convert_fusion) | data formatting | bytes 4194304 | tf_op jit(solution)/shard_map/reshape | solution.py:71
  71.3 2.9 %copy.100 = bf16[64,2,64,128]{3,0,2,1:T(8,128)(2,1)S(1)} copy(bf16[64,2,64,128]{3,2,1,0:T(8,128)(2,1)} %reshape.69) | data formatting | bytes 4194304 | tf_op jit(solution)/shard_map/reshape | solution.py:71
  74.3 0.7 gather_fusion
  75.0 1.1 select_bitcast_fusion
  76.2 7.6 %all-to-all-start = ((bf16[64,2,32,128]{3,0,1,2:T(8,128)(2,1)}), bf16[64,2,32,128]{3,0,1,2:T(8,128)(2,1)}, u32[]{:S(2)}, u32[]{:S(2)}) async-start(bf16[64,2,32,128]{3,0,1,2:T(8,128)(2,1)} %select_bitcast_fusion), calls=%async_computation | async-start | bytes 2097152 | tf_op jit(solution)/shard_map/all_to_all | solution.py:78
  83.8 16.5 %all-to-all-done = bf16[64,2,32,128]{3,0,1,2:T(8,128)(2,1)} async-done(((bf16[64,2,32,128]{3,0,1,2:T(8,128)(2,1)}), bf16[64,2,32,128]{3,0,1,2:T(8,128)(2,1)}, u32[]{:S(2)}, u32[]{:S(2)}) %all-to-all-start) | async-done | bytes 1048608 | tf_op jit(solution)/shard_map/all_to_all | solution.py:78
  100.4 1.5 copy.98
  101.8 0.2 slice.187
  102.1 0.2 slice.188
  102.3 0.6 copy-done.11
  102.9 1.3 bitcast_add_fusion.4
  104.2 0.2 slice.189
  104.4 0.2 slice.190
  104.6 1.3 bitcast_add_fusion.3
  105.9 0.2 slice.191
  106.1 0.2 slice.192
  106.2 1.3 bitcast_add_fusion.2
  107.5 0.2 slice.193
  107.7 0.1 slice.194
  107.8 2.2 %fusion.24 = bf16[64,32,2,128]{3,0,2,1:T(8,128)(2,1)} fusion(f32[64,32,2,128]{3,0,2,1:T(8,128)S(1)} %bitcast_add_fusion.2, f32[64,16,2,128]{3,0,2,1:T(8,128)S(1)} %slice.194, f32[64,24,2,128]{3,0,2,1:T(8,128)S(1)} %slice.193, f32[64]{0:T(128)S(1)} %get-tuple-element.35, f32[64]{0:T(128)S(1)} %get-tuple-element.36, f32[64]{0:T(128)S(1)} %get-tuple-element.25, ...), kind=kOutput, calls=%fused_computation.32 | convolution fusion | flops 73400320 | bytes 7882240 | tf_op jit(solution)/shard_map/oc,cfsn->ofsn/dot_general | solution.py:44
  110.0 4.9 %all-to-all-start.1 = ((bf16[64,32,2,128]{3,0,2,1:T(8,128)(2,1)}), bf16[64,32,2,128]{3,0,2,1:T(8,128)(2,1)}, u32[]{:S(2)}, u32[]{:S(2)}) async-start(bf16[64,32,2,128]{3,0,2,1:T(8,128)(2,1)} %fusion.24), calls=%async_computation.1 | async-start | bytes 2097152 | tf_op jit(solution)/shard_map/all_to_all | solution.py:76
  115.6 17.4 %all-to-all-done.1 = bf16[64,32,2,128]{3,0,2,1:T(8,128)(2,1)} async-done(((bf16[64,32,2,128]{3,0,2,1:T(8,128)(2,1)}), bf16[64,32,2,128]{3,0,2,1:T(8,128)(2,1)}, u32[]{:S(2)}, u32[]{:S(2)}) %all-to-all-start.1) | async-done | bytes 1048608 | tf_op jit(solution)/shard_map/all_to_all | solution.py:76
  133.0 1.3 copy.99
  134.3 1.3 bitcast_select_fusion
  135.5 4.0 %scatter_fusion = bf16[64,2,64,128]{3,0,2,1:T(8,128)(2,1)S(1)} fusion(bf16[64,2,64,128]{3,0,2,1:T(8,128)(2,1)S(1)} %copy.100, s32[32]{0:T(128)S(1)} %fusion.54, bf16[32,64,2,128]{3,1,2,0:T(8,128)(2,1)} %bitcast.163), kind=kCustom, calls=%fused_computation.1 | custom fusion | bytes 3145856 | tf_op jit(solution)/shard_map/scatter | solution.py:88
  139.6 2.7 %copy.101 = bf16[64,2,64,128]{3,2,1,0:T(8,128)(2,1)} copy(bf16[64,2,64,128]{3,0,2,1:T(8,128)(2,1)S(1)} %scatter_fusion) | data formatting | bytes 4194304 | tf_op jit(solution)/shard_map/scatter | solution.py:88
  142.3 4.1 %reshape.70 = bf16[64,2,32,256]{3,2,1,0:T(8,128)(2,1)} reshape(bf16[64,2,64,128]{3,2,1,0:T(8,128)(2,1)} %copy.101) | data formatting | bytes 4194304 | tf_op jit(solution)/shard_map/reshape | solution.py:89
  (42 shorter events, 1.0 us)
Async XLA Ops:
  3.0 6.4 %copy-start.12 = (s32[1,32]{1,0:T(1,128)S(1)}, s32[1,32]{1,0:T(1,128)}, u32[]{:S(2)}) copy-start(s32[1,32]{1,0:T(1,128)} %param.12) | copy-start | bytes 388
  3.0 6.4 %copy-start.8 = (bf16[9,64,8]{1,2,0:T(8,128)(2,1)S(1)}, bf16[9,64,8]{1,2,0:T(8,128)(2,1)}, u32[]{:S(2)}) copy-start(bf16[9,64,8]{1,2,0:T(8,128)(2,1)} %param.8) | copy-start | bytes 27652
  3.0 6.4 %copy-start = (bf16[64,2,32,256]{3,2,1,0:T(8,128)(2,1)S(1)}, bf16[64,2,32,256]{3,2,1,0:T(8,128)(2,1)}, u32[]{:S(2)}) copy-start(bf16[64,2,32,256]{3,2,1,0:T(8,128)(2,1)} %param.7) | copy-start | bytes 6291460
  5.6 7.3 %collective-permute-start = (bf16[64,2,32,1]{0,2,3,1:T(8,128)(2,1)S(1)}, bf16[64,2,32,1]{0,2,3,1:T(8,128)(2,1)S(1)}, u32[]{:S(2)}, u32[]{:S(2)}) collective-permute-start(bf16[64,2,32,1]{0,2,3,1:T(8,128)(2,1)S(1)} %copy.115), channel_id=1, source_target_pairs={{0,1},{1,2},{2,3},{3,4},{4,5},{5,6},{6,7},{8,9},{9,10},{10,11},{11... | collective-permute-start | bytes 24584 | tf_op jit(solution)/shard_map/ppermute | solution.py:17
  8.1 5.3 %collective-permute-start.1 = (bf16[64,2,32,1]{0,2,3,1:T(8,128)(2,1)S(1)}, bf16[64,2,32,1]{0,2,3,1:T(8,128)(2,1)S(1)}, u32[]{:S(2)}, u32[]{:S(2)}) collective-permute-start(bf16[64,2,32,1]{0,2,3,1:T(8,128)(2,1)S(1)} %copy.116), channel_id=1, source_target_pairs={{1,0},{2,1},{3,2},{4,3},{5,4},{6,5},{7,6},{9,8},{10,9},{11,10},{12... | collective-permute-start | bytes 24584 | tf_op jit(solution)/shard_map/ppermute | solution.py:19
  26.5 2.4 %copy-start.7 = (bf16[8,8,2,32,256]{4,1,0,3,2:T(8,128)(2,1)S(1)}, bf16[8,8,2,32,256]{4,1,0,3,2:T(8,128)(2,1)}, u32[]{:S(2)}) copy-start(bf16[8,8,2,32,256]{4,1,0,3,2:T(8,128)(2,1)} %get-tuple-element.8) | copy-start | bytes 6291460
  28.9 2.7 %copy-start.6 = (bf16[8,8,2,32,256]{4,1,0,3,2:T(8,128)(2,1)S(1)}, bf16[8,8,2,32,256]{4,1,0,3,2:T(8,128)(2,1)}, u32[]{:S(2)}) copy-start(bf16[8,8,2,32,256]{4,1,0,3,2:T(8,128)(2,1)} %get-tuple-element.9) | copy-start | bytes 6291460
  31.6 2.7 %copy-start.5 = (bf16[8,8,2,32,256]{4,1,0,3,2:T(8,128)(2,1)S(1)}, bf16[8,8,2,32,256]{4,1,0,3,2:T(8,128)(2,1)}, u32[]{:S(2)}) copy-start(bf16[8,8,2,32,256]{4,1,0,3,2:T(8,128)(2,1)} %get-tuple-element.10) | copy-start | bytes 6291460
  34.2 2.7 %copy-start.4 = (bf16[8,8,2,32,256]{4,1,0,3,2:T(8,128)(2,1)S(1)}, bf16[8,8,2,32,256]{4,1,0,3,2:T(8,128)(2,1)}, u32[]{:S(2)}) copy-start(bf16[8,8,2,32,256]{4,1,0,3,2:T(8,128)(2,1)} %get-tuple-element.11) | copy-start | bytes 6291460
  36.9 2.6 %copy-start.3 = (bf16[8,8,2,32,256]{4,1,0,3,2:T(8,128)(2,1)S(1)}, bf16[8,8,2,32,256]{4,1,0,3,2:T(8,128)(2,1)}, u32[]{:S(2)}) copy-start(bf16[8,8,2,32,256]{4,1,0,3,2:T(8,128)(2,1)} %get-tuple-element.12) | copy-start | bytes 6291460
  39.6 2.6 %copy-start.2 = (bf16[8,8,2,32,256]{4,1,0,3,2:T(8,128)(2,1)S(1)}, bf16[8,8,2,32,256]{4,1,0,3,2:T(8,128)(2,1)}, u32[]{:S(2)}) copy-start(bf16[8,8,2,32,256]{4,1,0,3,2:T(8,128)(2,1)} %get-tuple-element.13) | copy-start | bytes 6291460
  42.2 2.7 %copy-start.1 = (bf16[8,8,2,32,256]{4,1,0,3,2:T(8,128)(2,1)S(1)}, bf16[8,8,2,32,256]{4,1,0,3,2:T(8,128)(2,1)}, u32[]{:S(2)}) copy-start(bf16[8,8,2,32,256]{4,1,0,3,2:T(8,128)(2,1)} %get-tuple-element.6) | copy-start | bytes 6291460
  60.4 3.5 %copy-start.10 = (f32[64]{0:T(128)S(1)}, f32[64]{0:T(128)}, u32[]{:S(2)}) copy-start(f32[64]{0:T(128)} %param.9) | copy-start | bytes 772
  75.0 8.8 %copy-start.9 = (f32[4,3,64]{2,0,1:T(4,128)S(1)}, f32[4,3,64]{2,0,1:T(4,128)}, u32[]{:S(2)}) copy-start(f32[4,3,64]{2,0,1:T(4,128)} %param.10) | copy-start | bytes 9220
  76.2 24.2 %all-to-all-start = ((bf16[64,2,32,128]{3,0,1,2:T(8,128)(2,1)}), bf16[64,2,32,128]{3,0,1,2:T(8,128)(2,1)}, u32[]{:S(2)}, u32[]{:S(2)}) async-start(bf16[64,2,32,128]{3,0,1,2:T(8,128)(2,1)} %select_bitcast_fusion), calls=%async_computation | async-start | bytes 2097152 | tf_op jit(solution)/shard_map/all_to_all | solution.py:78
  102.1 0.8 copy-start.11
  110.0 23.0 %all-to-all-start.1 = ((bf16[64,32,2,128]{3,0,2,1:T(8,128)(2,1)}), bf16[64,32,2,128]{3,0,2,1:T(8,128)(2,1)}, u32[]{:S(2)}, u32[]{:S(2)}) async-start(bf16[64,32,2,128]{3,0,2,1:T(8,128)(2,1)} %fusion.24), calls=%async_computation.1 | async-start | bytes 2097152 | tf_op jit(solution)/shard_map/all_to_all | solution.py:76
where the time goes:
time: 149 us; the launch traced here: 146 us
  local copies, waits for them, and re-layouts  47.1 us (32%)
  matrix products  39.9 us (27%)
  waiting for transfers between devices  33.9 us (23%)
  starting transfers between devices  15.1 us (10%)
  other arithmetic  9.39 us (6%)
    dot_general x9, matrix products, spatial(): jnp.einsum('goi,gifrw->gofrw', kernel, window, preferred_element_type=jnp...  33.9 us
    all_to_all x1, waiting for transfers between devices, on_device(): lax.all_to_all(temporal(lax.all_to_all(picked, 'frame', split_axis=2, con...  17.4 us
    all_to_all x1, waiting for transfers between devices, on_device(): lax.all_to_all(picked, 'frame', split_axis=2, concat_axis=1, tiled=True)  16.5 us
    slice x1, local copies, waits for them, and re-layouts, spatial(): grouped[:, :, :, tap_row:tap_row + height, tap_col:tap_col + columns]  7.92 us
    all_to_all x1, starting transfers between devices, on_device(): lax.all_to_all(picked, 'frame', split_axis=2, concat_axis=1, tiled=True)  7.62 us
    reshape x2, local copies, waits for them, and re-layouts, on_device(): blocks = hidden.reshape(channels, frames, height * (columns // 128), 128)  7.03 us
    unnamed x29, local copies, waits for them, and re-layouts  6.94 us
    scatter x2, local copies, waits for them, and re-layouts, on_device(): blocks = blocks.at[:, :, block_ids].set(chosen)  6.73 us
  transfers between devices with their start and end apart: 4, of which 2 were waited for; matrix products, arithmetic and copies ran while one was open for 4% of the time, Pallas kernels for 0%

commit v1 on v0

v1 whole, which is shorter than its diff:
```python
import functools

import jax
import jax.numpy as jnp
from jax import lax
from jax.experimental import pallas as pl
from jax.experimental.pallas import tpu as pltpu
from jax.sharding import PartitionSpec as P

MESH = pl.DeviceIdType.MESH
F32 = jnp.float32
BF16 = jnp.bfloat16

HOPS = (
    (2, 2), (2, 1), (2, 3), (1, 2), (3, 2), (2, 0), (0, 2),
    (1, 1), (3, 3), (1, 3), (3, 1), (1, 0), (3, 0), (0, 1), (0, 3),
)


def rows(shape):
    return lax.broadcasted_iota(jnp.int32, shape, 0)


def cols(shape):
    return lax.broadcasted_iota(jnp.int32, shape, 1)


def one_hot(mask):
    return jnp.where(mask, 1.0, 0.0).astype(BF16)


def dot(lhs, rhs, contract=((1,), (0,))):
    return lax.dot_general(lhs, rhs, (contract, ((), ())), preferred_element_type=F32)


def gated(half):
    return half + half * jnp.tanh(half)


def kernel(
    grid_hbm, weight_ref, bias_ref, depth_ref, point_ref, occupied_ref, count_ref,
    out_ref,
    cells, wide, lanes, band, slot_band, pick, place, covered, mix, taps, bias_col, half_col,
    edge_out, edge_in, hidden, outgoing, incoming, state, answer, returned,
    load_sem, edge_send, edge_recv, send_sems, recv_sems,
):
    me = lax.axis_index("frame")
    tile = lax.axis_index("tile")
    row, col = me // 4, me % 4
    right, left = {"tile": (tile + 1) % 8}, {"tile": (tile + 7) % 8}

    def peer(hop):
        return ((row + hop[0]) % 4) * 4 + (col + hop[1]) % 4

    barrier = pltpu.get_barrier_semaphore()
    for neighbour in (right, left):
        pl.semaphore_signal(barrier, inc=1, device_id=neighbour, device_id_type=MESH)
    for hop in HOPS:
        pl.semaphore_signal(barrier, inc=1, device_id={"frame": peer(hop)}, device_id_type=MESH)
    load = pltpu.make_async_copy(grid_hbm, cells, load_sem)
    load.start()

    spread = one_hot((cols((8, 256)) >> 5) == rows((8, 256)))
    for tap in range(9):
        lanes[tap] = 0.5 * dot(weight_ref[tap], spread, ((0,), (0,)))
    delta = (cols((32, 256)) & 31) - rows((32, 256))

    @pl.loop(0, 8)
    def _(g):
        for dc in range(3):
            for o in range(8):
                value = jnp.zeros((32, 256), F32)
                for dr in range(3):
                    line = lanes[3 * dr + dc, pl.ds(8 * g + o, 1), :]
                    value = jnp.where(delta == dr - 1, line, value)
                band[g, o * 32 : (o + 1) * 32, dc * 256 : (dc + 1) * 256] = value.astype(BF16)

    listed = occupied_ref[...]
    row_of = (listed >> 1).astype(F32)
    half_of = (listed & 1).astype(F32)
    own = cols((256, 32)) == (rows((256, 32)) >> 3)
    row_col = jnp.sum(jnp.where(own, row_of, 0.0), axis=1, keepdims=True)
    half_col[...] = jnp.broadcast_to(jnp.sum(jnp.where(own, half_of, 0.0), axis=1, keepdims=True), (256, 128))
    r2, c2 = rows((256, 256)), cols((256, 256))
    pick[...] = one_hot(((r2 & 7) == (c2 >> 5)) & ((c2 & 31).astype(F32) == row_col))
    expand = one_hot((cols((32, 256)) >> 3) == rows((32, 256)))
    row_lane = dot(jnp.broadcast_to(row_of, (8, 32)).astype(BF16), expand)[0:1]
    half_lane = dot(jnp.broadcast_to(half_of, (8, 32)).astype(BF16), expand)[0:1]
    live = (c2 >> 3) < count_ref[0]
    target = ((r2 >> 5) == (c2 & 7)) & ((r2 & 31).astype(F32) == row_lane) & live
    for h in range(2):
        chosen = jnp.where(target & (half_lane == float(h)), 1.0, 0.0)
        place[h * 256 : (h + 1) * 256, :] = chosen.astype(BF16)
        covered[:, h * 128 : (h + 1) * 128] = jnp.broadcast_to(jnp.sum(chosen, axis=1, keepdims=True), (256, 128))

    @pl.loop(0, 8)
    def _(g):
        slot_band[g] = dot(pick[...], band[g]).astype(BF16)

    diagonal = rows((64, 64)) == cols((64, 64))
    bias_half = jnp.sum(jnp.where(diagonal, 0.5 * bias_ref[...], 0.0), axis=1, keepdims=True)
    bias_col[...] = jnp.broadcast_to(bias_half, (64, 256))
    for layer in range(4):
        for j in range(3):
            line = 0.5 * depth_ref[j, layer : layer + 1, :]
            column = jnp.sum(jnp.where(diagonal, line, 0.0), axis=1, keepdims=True)
            taps[3 * layer + j] = jnp.broadcast_to(column, (64, 128))
    repeat = one_hot((rows((256, 64)) & 63) == cols((256, 64)))
    for layer in range(4):
        tall = dot(repeat, point_ref[layer]).astype(BF16)
        full = dot(tall, repeat, ((1,), (1,)))
        mix[layer] = jnp.where((r2 >> 6) == (c2 >> 6), full, 0.0).astype(BF16)

    load.wait()
    r3, c3 = rows((32, 256)), cols((32, 256))

    def edges(n, total):
        block = cells[pl.ds(8 * (n // 2), 8), n % 2].reshape(256, 256)
        wanted = ((r3 == n) & (c3 == 255)) | ((r3 == 16 + n) & (c3 == 0))
        return total + dot(one_hot(wanted), block, ((1,), (1,)))

    both = lax.fori_loop(0, 16, edges, jnp.zeros((32, 256), F32)).astype(BF16)
    edge_out[0] = both[:16]
    edge_out[1] = both[16:]
    pl.semaphore_wait(barrier, 17)
    edge_copies = []
    for side, neighbour in enumerate((right, left)):
        copy = pltpu.make_async_remote_copy(
            src_ref=edge_out.at[side],
            dst_ref=edge_in.at[side],
            send_sem=edge_send.at[side],
            recv_sem=edge_recv.at[side],
            device_id=neighbour,
            device_id_type=MESH,
        )
        copy.start()
        edge_copies.append(copy)

    lane = cols((256, 256))

    @pl.loop(0, 16)
    def _(n):
        block = cells[pl.ds(8 * (n // 2), 8), n % 2].reshape(256, 256)
        wide[n, 256:512] = block
        block = block.astype(F32)
        wide[n, 0:256] = jnp.where(lane == 0, 0.0, pltpu.roll(block, 1, 1)).astype(BF16)
        wide[n, 512:768] = jnp.where(lane == 255, 0.0, pltpu.roll(block, 255, 1)).astype(BF16)

    for copy in edge_copies:
        copy.wait()
    arrived = edge_in[...].reshape(32, 256).astype(F32)
    there = ((r3 < 16) & (tile > 0)) | ((r3 >= 16) & (tile < 7))
    halo = jnp.where(there, arrived, 0.0).T.astype(BF16)

    @pl.loop(0, 16)
    def _(n):
        put = one_hot(((r3 == n) & (c3 == 0)) | ((r3 == 16 + n) & (c3 == 255)))
        fix = dot(halo, put).astype(BF16)
        wide[n, 0:256, 0:128] += fix[:, :128]
        wide[n, 512:768, 128:256] += fix[:, 128:]

    def slots(s):
        lo = 128 * s

        @pl.loop(0, 4)
        def _(pair):
            second = half_col[lo : lo + 128] > 0.5
            for f in range(2):
                parts = []
                for e in range(2):
                    g = 2 * pair + e
                    act = dot(slot_band[g, lo : lo + 128, :], wide[2 * g + f])
                    plain = dot(pick[lo : lo + 128, :], wide[2 * g + f, 256:512])
                    act = jnp.where(second, act[:, 128:], act[:, :128]).reshape(16, 8, 128)
                    plain = jnp.where(second, plain[:, 128:], plain[:, :128]).reshape(16, 8, 128)
                    act = act + bias_col[pl.ds(8 * g, 8), 0:128]
                    parts.append(plain + gated(act))
                joined = jnp.concatenate(parts, axis=1).astype(BF16)
                outgoing[16 * s : 16 * s + 16, f, pl.ds(16 * pair, 16), :] = joined

    copies = []

    def send(stage, source, target):
        for hop in HOPS:
            to = peer(hop)
            copy = pltpu.make_async_remote_copy(
                src_ref=source(to),
                dst_ref=target,
                send_sem=send_sems.at[stage],
                recv_sem=recv_sems.at[stage],
                device_id={"frame": to},
                device_id_type=MESH,
            )
            copy.start()

    def whole(stage, ref):
        return pltpu.make_async_remote_copy(
            src_ref=ref,
            dst_ref=ref,
            send_sem=send_sems.at[stage],
            recv_sem=recv_sems.at[stage],
            device_id={"frame": peer(HOPS[0])},
            device_id_type=MESH,
        )

    for s in range(2):
        slots(s)
        send(s, lambda to, s=s: outgoing.at[16 * s + to], incoming.at[s, me])
        incoming[s, me] = outgoing[16 * s + me]

    @pl.loop(0, 8)
    def _(g):
        for f in range(2):
            act = dot(band[g], wide[2 * g + f])
            for o in range(8):
                half = act[o * 32 : (o + 1) * 32] + bias_col[pl.ds(8 * g + o, 1), :]
                value = cells[8 * g + o, f].astype(F32) + gated(half)
                hidden[8 * g + o, f] = value.astype(BF16)

    def temporal(s):
        state[0:16] = jnp.zeros((16, 64, 128), F32)

        @pl.loop(0, 16)
        def _(p):
            state[pl.ds(16 + 2 * p, 2)] = incoming[s, p].astype(F32)

        for layer in range(4):
            d = 2**layer

            @pl.loop(0, 4)
            def _(i):
                base = 40 - 8 * i
                now = state[pl.ds(base, 8)]
                half = taps[3 * layer] * now
                half = half + taps[3 * layer + 1] * state[pl.ds(base - d, 8)]
                half = half + taps[3 * layer + 2] * state[pl.ds(base - 2 * d, 8)]
                squashed = gated(half).astype(BF16)
                pair = [squashed[0:4].reshape(256, 128), squashed[4:8].reshape(256, 128)]
                mixed = dot(mix[layer], jnp.concatenate(pair, axis=1))
                for h in range(2):
                    new = now[4 * h : 4 * h + 4] + mixed[:, 128 * h : 128 * h + 128].reshape(4, 64, 128)
                    if layer < 3:
                        state[pl.ds(base + 4 * h, 4)] = new
                    else:
                        answer[s, pl.ds(12 - 4 * i + 2 * h, 2)] = new.reshape(2, 2, 64, 128).astype(BF16)

    for s in range(2):
        whole(s, incoming.at[s, pl.ds(0, 15)]).wait_recv()
        temporal(s)
        send(2 + s, lambda to, s=s: answer.at[s, to], returned.at[16 * s + me])
        returned[16 * s + me] = answer[s, me]

    for s in range(2):
        whole(2 + s, returned.at[pl.ds(0, 15)]).wait_recv()

    @pl.loop(0, 4)
    def _(pair):
        split = [returned[:, f, pl.ds(16 * pair, 16), :].astype(F32) for f in range(2)]
        for e in range(2):
            g = 2 * pair + e
            both = [part[:, 8 * e : 8 * e + 8].reshape(256, 128) for part in split]
            value = dot(place[...], jnp.concatenate(both, axis=1).astype(BF16))
            for f in range(2):
                for h in range(2):
                    span = slice(128 * h, 128 * h + 128)
                    new = value[256 * h : 256 * h + 256, 128 * f : 128 * f + 128]
                    old = hidden[pl.ds(8 * g, 8), f, :, span].reshape(256, 128).astype(F32)
                    new = jnp.where(covered[:, span] > 0.5, new, old)
                    out_ref[pl.ds(8 * g, 8), f, :, span] = new.reshape(8, 32, 128).astype(BF16)

    for s in range(2):
        whole(s, outgoing.at[pl.ds(0, 15)]).wait_send()
        whole(2 + s, answer.at[s, pl.ds(0, 15)]).wait_send()


def on_device(grid, conv_weight, conv_bias, depth_kernel, point_weight, occupied, counts):
    vmem = pl.BlockSpec(memory_space=pltpu.VMEM)
    buffers = [
        ((64, 2, 32, 256), BF16),
        ((16, 768, 256), BF16),
        ((9, 64, 256), F32),
        ((8, 256, 768), BF16),
        ((8, 256, 768), BF16),
        ((256, 256), BF16),
        ((512, 256), BF16),
        ((256, 256), F32),
        ((4, 256, 256), BF16),
        ((12, 64, 128), F32),
        ((64, 256), F32),
        ((256, 128), F32),
        ((2, 16, 256), BF16),
        ((2, 16, 256), BF16),
        ((64, 2, 32, 256), BF16),
        ((32, 2, 64, 128), BF16),
        ((2, 16, 2, 64, 128), BF16),
        ((48, 64, 128), F32),
        ((2, 16, 2, 64, 128), BF16),
        ((32, 2, 64, 128), BF16),
    ]
    return pl.pallas_call(
        kernel,
        out_shape=jax.ShapeDtypeStruct(grid.shape, grid.dtype),
        in_specs=[pl.BlockSpec(memory_space=pl.ANY)] + [vmem] * 5 + [pl.BlockSpec(memory_space=pltpu.SMEM)],
        out_specs=vmem,
        scratch_shapes=[pltpu.VMEM(shape, kind) for shape, kind in buffers]
        + [
            pltpu.SemaphoreType.DMA,
            pltpu.SemaphoreType.DMA((2,)),
            pltpu.SemaphoreType.DMA((2,)),
            pltpu.SemaphoreType.DMA((4,)),
            pltpu.SemaphoreType.DMA((4,)),
        ],
        compiler_params=pltpu.CompilerParams(
            collective_id=0, has_side_effects=True, vmem_limit_bytes=56 * 1024 * 1024
        ),
        cost_estimate=pl.CostEstimate(flops=4_000_000_000, bytes_accessed=4 << 20, transcendentals=3 << 20),
    )(
        grid,
        conv_weight.transpose(0, 2, 1),
        conv_bias.reshape(1, 64),
        depth_kernel.transpose(1, 0, 2),
        point_weight,
        occupied,
        counts,
    )


def solution(mesh):
    placed = (P(None, "frame", None, "tile"), P(), P(), P(), P(), P("tile", None), P("tile"))
    return jax.shard_map(
        on_device,
        mesh=mesh,
        in_specs=placed,
        out_specs=P(None, "frame", None, "tile"),
        check_vma=False,
    )
```

time: 149 us -> 52.8 us (0.35); the launches traced: 146 us -> 52.5 us
  Pallas kernels: 0 us -> 48.6 us
  local copies, waits for them, and re-layouts: 47.1 us -> 3.22 us
  matrix products: 39.9 us -> 0 us
  waiting for transfers between devices: 33.9 us -> 0 us
  starting transfers between devices: 15.1 us -> 0 us
  other arithmetic: 9.39 us -> 0 us
    pallas_call x0 -> x1, Pallas kernels: none -> 48.6 us  [on_device(): pl.pallas_call(kernel, out_shape=jax.ShapeDtypeStruct(grid.shape, grid.dt...]
    dot_general x13 -> x0, matrix products: 39.9 us -> none  [the longest x9 33.9 us: spatial(): jnp.einsum('goi,gifrw->gofrw', kernel, window, preferred_element_type=jnp...]
    all_to_all x2 -> x0, waiting for transfers between devices: 33.9 us -> none  [the longest x1 17.4 us: on_device(): lax.all_to_all(temporal(lax.all_to_all(picked, 'frame', split_axis=2, con...]
    slice x20 -> x0, local copies, waits for them, and re-layouts: 13.4 us -> none  [the longest x1 7.92 us: spatial(): grouped[:, :, :, tap_row:tap_row + height, tap_col:tap_col + columns]]
    all_to_all x2 -> x0, starting transfers between devices: 12.5 us -> none  [the longest x1 7.62 us: on_device(): lax.all_to_all(picked, 'frame', split_axis=2, concat_axis=1, tiled=True)]
    reshape x3 -> x0, local copies, waits for them, and re-layouts: 11.1 us -> none  [the longest x2 7.03 us: on_device(): blocks = hidden.reshape(channels, frames, height * (columns // 128), 128)]
    scatter x2 -> x0, local copies, waits for them, and re-layouts: 6.73 us -> none  [on_device(): blocks = blocks.at[:, :, block_ids].set(chosen)]
    unnamed x29 -> x1, local copies, waits for them, and re-layouts: 6.94 us -> 3.22 us
  transfers between devices with their start and end apart: 4 -> 0, of which waited for: 2 -> 0; matrix products, arithmetic and copies ran while one was open for 4% -> 0% of each run, Pallas kernels for 0% -> 0%
where the time goes in v1:
time: 52.8 us; the launch traced here: 52.5 us
  Pallas kernels  48.6 us (92%)
  local copies, waits for them, and re-layouts  3.22 us (6%)
  between operations  0.66 us (1%)
    pallas_call x1, Pallas kernels, on_device(): pl.pallas_call(kernel, out_shape=jax.ShapeDtypeStruct(grid.shape, grid.dt...  48.6 us
    unnamed x1, local copies, waits for them, and re-layouts  3.22 us

profile of v1, /device:TPU:0, one launch (start us, length us, event | category | flops | bytes accessed | tf_op | source)
XLA Modules:
  0.0 52.5 jit_solution(4473107589965177514)
XLA Ops:
  0.7 48.6 %shard_map.73 = bf16[64,2,32,256]{3,2,1,0:T(8,128)(2,1)} custom-call(bf16[64,2,32,256]{3,2,1,0:T(8,128)(2,1)} %grid_hbm.1, bf16[9,8,64]{2,1,0:T(8,128)(2,1)} %bitcast.3, f32[1,64]{1,0:T(1,128)} %bitcast.5, f32[3,4,64]{2,1,0:T(4,128)} %bitcast.4, bf16[4,64,64]{2,1,0:T(8,128)(2,1)} %point_ref.1, s32[1,32]{1,0:T(1,128)} %occupied_ref.1, s32[1]{0:T(128)S(6)} %copy.9.count_ref), custom_call_target="tpu_custom_call" | custom-call | flops 4000000000 | bytes 4194304 | tf_op jit(solution)/shard_map/pallas_call | solution.py:300
  49.3 3.2 %copy.10 = bf16[64,2,32,256]{3,2,1,0:T(8,128)(2,1)} copy(bf16[64,2,32,256]{3,2,1,0:T(8,128)(2,1)} %shard_map.73) | data formatting | bytes 4194304

commit v2 on v1

--- a/solution.py
+++ b/solution.py
@@ -10,6 +10,7 @@
 MESH = pl.DeviceIdType.MESH
 F32 = jnp.float32
 BF16 = jnp.bfloat16
+UNROLL = 4
 
 HOPS = (
     (2, 2), (2, 1), (2, 3), (1, 2), (3, 2), (2, 0), (0, 2),
@@ -38,11 +39,12 @@
 
 
 def kernel(
-    grid_hbm, weight_ref, bias_ref, depth_ref, point_ref, occupied_ref, count_ref,
+    grid_hbm, weight_hbm, bias_hbm, depth_hbm, point_hbm, occupied_hbm, count_hbm,
     out_ref,
-    cells, wide, lanes, band, slot_band, pick, place, covered, mix, taps, bias_col, half_col,
+    weight_ref, bias_ref, depth_ref, point_ref, occupied_ref, count_ref, cells, wide, lanes, band,
+    slot_band, pick, place, covered, mix, taps, bias_col, row_col, half_col,
     edge_out, edge_in, hidden, outgoing, incoming, state, answer, returned,
-    load_sem, edge_send, edge_recv, send_sems, recv_sems,
+    load_sems, edge_send, edge_recv, send_sems, recv_sems,
 ):
     me = lax.axis_index("frame")
     tile = lax.axis_index("tile")
@@ -57,13 +59,77 @@
         pl.semaphore_signal(barrier, inc=1, device_id=neighbour, device_id_type=MESH)
     for hop in HOPS:
         pl.semaphore_signal(barrier, inc=1, device_id={"frame": peer(hop)}, device_id_type=MESH)
-    load = pltpu.make_async_copy(grid_hbm, cells, load_sem)
-    load.start()
+    sources = (grid_hbm, weight_hbm, bias_hbm, depth_hbm, point_hbm, occupied_hbm, count_hbm)
+    targets = (cells, weight_ref, bias_ref, depth_ref, point_ref, occupied_ref, count_ref)
+    loads = []
+    for i, (source, target) in enumerate(zip(sources, targets)):
+        loads.append(pltpu.make_async_copy(source, target, load_sems.at[i]))
+        loads[i].start()
+
+    loads[0].wait()
+    lane, lane_wide = cols((256, 128)), cols((256, 256))
+    nought = jnp.zeros((256, 256), BF16)
+
+    def shift(n, edge):
+        block = cells[pl.ds(8 * (n // 2), 8), n % 2].reshape(256, 256)
+        wide[n, 256:512] = block
+        wide[n, 0:256] = jnp.where(lane_wide == 0, nought, pltpu.roll(block, 1, 1))
+        wide[n, 512:768] = jnp.where(lane_wide == 255, nought, pltpu.roll(block, 255, 1))
+        edge = jnp.where(lane == n, pltpu.roll(block[:, 128:], n + 1, 1), edge)
+        return jnp.where(lane == 16 + n, pltpu.roll(block[:, :128], 16 + n, 1), edge)
+
+    edge_out[...] = lax.fori_loop(0, 16, shift, nought[:, :128], unroll=UNROLL)
+
+    for load in loads[1:]:
+        load.wait()
+    r2, c2 = rows((256, 256)), cols((256, 256))
+    listed = occupied_ref[...]
+    row_of = (listed >> 1).astype(F32)
+    half_of = (listed & 1).astype(F32)
+    own = cols((256, 32)) == (rows((256, 32)) >> 3)
+    row_here = jnp.sum(jnp.where(own, row_of, 0.0), axis=1, keepdims=True)
+    row_col[...] = jnp.broadcast_to(row_here, (256, 256))
+    half_col[...] = jnp.broadcast_to(jnp.sum(jnp.where(own, half_of, 0.0), axis=1, keepdims=True), (256, 128))
+    pick[...] = one_hot(((r2 & 7) == (c2 >> 5)) & ((c2 & 31).astype(F32) == row_here))
+    diagonal = rows((64, 64)) == cols((64, 64))
+    bias_half = jnp.sum(jnp.where(diagonal, 0.5 * bias_ref[...], 0.0), axis=1, keepdims=True)
+    bias_col[...] = jnp.broadcast_to(bias_half, (64, 256))
 
     spread = one_hot((cols((8, 256)) >> 5) == rows((8, 256)))
     for tap in range(9):
         lanes[tap] = 0.5 * dot(weight_ref[tap], spread, ((0,), (0,)))
-    delta = (cols((32, 256)) & 31) - rows((32, 256))
+    row_lanes = (cols((8, 256)) & 31).astype(F32)
+
+    @pl.loop(0, 16)
+    def _(pair):
+        start = pl.multiple_of(16 * pair, 16)
+        delta = [row_lanes - row_col[pl.ds(start + 8 * k, 8)] for k in range(2)]
+        for g in range(8):
+            for dc in range(3):
+                parts = []
+                for k in range(2):
+                    value = jnp.zeros((8, 256), F32)
+                    for dr in range(3):
+                        value = jnp.where(delta[k] == dr - 1.0, lanes[3 * dr + dc, 8 * g : 8 * g + 8], value)
+                    parts.append(value)
+                both = jnp.concatenate(parts, axis=0).astype(BF16)
+                slot_band[g, pl.ds(start, 16), dc * 256 : (dc + 1) * 256] = both
+
+    pl.semaphore_wait(barrier, 17)
+    edge_copies = []
+    for side, neighbour in enumerate((right, left)):
+        copy = pltpu.make_async_remote_copy(
+            src_ref=edge_out,
+            dst_ref=edge_in.at[side],
+            send_sem=edge_send.at[side],
+            recv_sem=edge_recv.at[side],
+            device_id=neighbour,
+            device_id_type=MESH,
+        )
+        copy.start()
+        edge_copies.append(copy)
+
+    offset = (cols((32, 256)) & 31) - rows((32, 256))
 
     @pl.loop(0, 8)
     def _(g):
@@ -72,17 +138,9 @@
                 value = jnp.zeros((32, 256), F32)
                 for dr in range(3):
                     line = lanes[3 * dr + dc, pl.ds(8 * g + o, 1), :]
-                    value = jnp.where(delta == dr - 1, line, value)
+                    value = jnp.where(offset == dr - 1, line, value)
                 band[g, o * 32 : (o + 1) * 32, dc * 256 : (dc + 1) * 256] = value.astype(BF16)
 
-    listed = occupied_ref[...]
-    row_of = (listed >> 1).astype(F32)
-    half_of = (listed & 1).astype(F32)
-    own = cols((256, 32)) == (rows((256, 32)) >> 3)
-    row_col = jnp.sum(jnp.where(own, row_of, 0.0), axis=1, keepdims=True)
-    half_col[...] = jnp.broadcast_to(jnp.sum(jnp.where(own, half_of, 0.0), axis=1, keepdims=True), (256, 128))
-    r2, c2 = rows((256, 256)), cols((256, 256))
-    pick[...] = one_hot(((r2 & 7) == (c2 >> 5)) & ((c2 & 31).astype(F32) == row_col))
     expand = one_hot((cols((32, 256)) >> 3) == rows((32, 256)))
     row_lane = dot(jnp.broadcast_to(row_of, (8, 32)).astype(BF16), expand)[0:1]
     half_lane = dot(jnp.broadcast_to(half_of, (8, 32)).astype(BF16), expand)[0:1]
@@ -93,13 +151,6 @@
         place[h * 256 : (h + 1) * 256, :] = chosen.astype(BF16)
         covered[:, h * 128 : (h + 1) * 128] = jnp.broadcast_to(jnp.sum(chosen, axis=1, keepdims=True), (256, 128))
 
-    @pl.loop(0, 8)
-    def _(g):
-        slot_band[g] = dot(pick[...], band[g]).astype(BF16)
-
-    diagonal = rows((64, 64)) == cols((64, 64))
-    bias_half = jnp.sum(jnp.where(diagonal, 0.5 * bias_ref[...], 0.0), axis=1, keepdims=True)
-    bias_col[...] = jnp.broadcast_to(bias_half, (64, 256))
     for layer in range(4):
         for j in range(3):
             line = 0.5 * depth_ref[j, layer : layer + 1, :]
@@ -111,58 +162,24 @@
         full = dot(tall, repeat, ((1,), (1,)))
         mix[layer] = jnp.where((r2 >> 6) == (c2 >> 6), full, 0.0).astype(BF16)
 
-    load.wait()
-    r3, c3 = rows((32, 256)), cols((32, 256))
-
-    def edges(n, total):
-        block = cells[pl.ds(8 * (n // 2), 8), n % 2].reshape(256, 256)
-        wanted = ((r3 == n) & (c3 == 255)) | ((r3 == 16 + n) & (c3 == 0))
-        return total + dot(one_hot(wanted), block, ((1,), (1,)))
-
-    both = lax.fori_loop(0, 16, edges, jnp.zeros((32, 256), F32)).astype(BF16)
-    edge_out[0] = both[:16]
-    edge_out[1] = both[16:]
-    pl.semaphore_wait(barrier, 17)
-    edge_copies = []
-    for side, neighbour in enumerate((right, left)):
-        copy = pltpu.make_async_remote_copy(
-            src_ref=edge_out.at[side],
-            dst_ref=edge_in.at[side],
-            send_sem=edge_send.at[side],
-            recv_sem=edge_recv.at[side],
-            device_id=neighbour,
-            device_id_type=MESH,
-        )
-        copy.start()
-        edge_copies.append(copy)
-
-    lane = cols((256, 256))
-
-    @pl.loop(0, 16)
-    def _(n):
-        block = cells[pl.ds(8 * (n // 2), 8), n % 2].reshape(256, 256)
-        wide[n, 256:512] = block
-        block = block.astype(F32)
-        wide[n, 0:256] = jnp.where(lane == 0, 0.0, pltpu.roll(block, 1, 1)).astype(BF16)
-        wide[n, 512:768] = jnp.where(lane == 255, 0.0, pltpu.roll(block, 255, 1)).astype(BF16)
-
     for copy in edge_copies:
         copy.wait()
-    arrived = edge_in[...].reshape(32, 256).astype(F32)
-    there = ((r3 < 16) & (tile > 0)) | ((r3 >= 16) & (tile < 7))
-    halo = jnp.where(there, arrived, 0.0).T.astype(BF16)
-
-    @pl.loop(0, 16)
-    def _(n):
-        put = one_hot(((r3 == n) & (c3 == 0)) | ((r3 == 16 + n) & (c3 == 255)))
-        fix = dot(halo, put).astype(BF16)
-        wide[n, 0:256, 0:128] += fix[:, :128]
-        wide[n, 512:768, 128:256] += fix[:, 128:]
+    from_left = jnp.where(tile > 0, edge_in[0], nought[:, :128])
+    from_right = jnp.where(tile < 7, edge_in[1], nought[:, :128])
+
+    def fix(n, carry):
+        old = wide[n, 0:256, 0:128]
+        wide[n, 0:256, 0:128] = jnp.where(lane == 0, pltpu.roll(from_left, (128 - n) % 128, 1), old)
+        old = wide[n, 512:768, 128:256]
+        wide[n, 512:768, 128:256] = jnp.where(lane == 127, pltpu.roll(from_right, 111 - n, 1), old)
+        return carry
+
+    lax.fori_loop(0, 16, fix, 0, unroll=UNROLL)
 
     def slots(s):
         lo = 128 * s
 
-        @pl.loop(0, 4)
+        @pl.loop(0, 4, unroll=2)
         def _(pair):
             second = half_col[lo : lo + 128] > 0.5
             for f in range(2):
@@ -208,7 +225,7 @@
         send(s, lambda to, s=s: outgoing.at[16 * s + to], incoming.at[s, me])
         incoming[s, me] = outgoing[16 * s + me]
 
-    @pl.loop(0, 8)
+    @pl.loop(0, 8, unroll=2)
     def _(g):
         for f in range(2):
             act = dot(band[g], wide[2 * g + f])
@@ -220,14 +237,14 @@
     def temporal(s):
         state[0:16] = jnp.zeros((16, 64, 128), F32)
 
-        @pl.loop(0, 16)
+        @pl.loop(0, 16, unroll=4)
         def _(p):
             state[pl.ds(16 + 2 * p, 2)] = incoming[s, p].astype(F32)
 
         for layer in range(4):
             d = 2**layer
 
-            @pl.loop(0, 4)
+            @pl.loop(0, 4, unroll=4)
             def _(i):
                 base = 40 - 8 * i
                 now = state[pl.ds(base, 8)]
@@ -253,7 +270,7 @@
     for s in range(2):
         whole(2 + s, returned.at[pl.ds(0, 15)]).wait_recv()
 
-    @pl.loop(0, 4)
+    @pl.loop(0, 4, unroll=2)
     def _(pair):
         split = [returned[:, f, pl.ds(16 * pair, 16), :].astype(F32) for f in range(2)]
         for e in range(2):
@@ -274,7 +291,6 @@
 
 
 def on_device(grid, conv_weight, conv_bias, depth_kernel, point_weight, occupied, counts):
-    vmem = pl.BlockSpec(memory_space=pltpu.VMEM)
     buffers = [
         ((64, 2, 32, 256), BF16),
         ((16, 768, 256), BF16),
@@ -287,9 +303,10 @@
         ((4, 256, 256), BF16),
         ((12, 64, 128), F32),
         ((64, 256), F32),
+        ((256, 256), F32),
         ((256, 128), F32),
-        ((2, 16, 256), BF16),
-        ((2, 16, 256), BF16),
+        ((256, 128), BF16),
+        ((2, 256, 128), BF16),
         ((64, 2, 32, 256), BF16),
         ((32, 2, 64, 128), BF16),
         ((2, 16, 2, 64, 128), BF16),
@@ -300,11 +317,19 @@
     return pl.pallas_call(
         kernel,
         out_shape=jax.ShapeDtypeStruct(grid.shape, grid.dtype),
-        in_specs=[pl.BlockSpec(memory_space=pl.ANY)] + [vmem] * 5 + [pl.BlockSpec(memory_space=pltpu.SMEM)],
-        out_specs=vmem,
-        scratch_shapes=[pltpu.VMEM(shape, kind) for shape, kind in buffers]
+        in_specs=[pl.BlockSpec(memory_space=pltpu.HBM)] * 7,
+        out_specs=pl.BlockSpec(memory_space=pltpu.VMEM),
+        scratch_shapes=[
+            pltpu.VMEM((9, 8, 64), BF16),
+            pltpu.VMEM((1, 64), F32),
+            pltpu.VMEM((3, 4, 64), F32),
+            pltpu.VMEM((4, 64, 64), BF16),
+            pltpu.VMEM((1, 32), jnp.int32),
+            pltpu.SMEM((1,), jnp.int32),
+        ]
+        + [pltpu.VMEM(shape, kind) for shape, kind in buffers]
         + [
-            pltpu.SemaphoreType.DMA,
+            pltpu.SemaphoreType.DMA((7,)),
             pltpu.SemaphoreType.DMA((2,)),
             pltpu.SemaphoreType.DMA((2,)),
             pltpu.SemaphoreType.DMA((4,)),

time: 52.8 us -> 46.3 us (0.88)
  Pallas kernels: 48.6 us -> 42.1 us
    pallas_call x1, Pallas kernels: 48.6 us -> 42.1 us  [on_device(): pl.pallas_call(kernel, out_shape=jax.ShapeDtypeStruct(grid.shape, grid.dt...]
where the time goes in v2:
time: 46.3 us; the launch traced here: 46 us
  Pallas kernels  42.1 us (91%)
  local copies, waits for them, and re-layouts  3.22 us (7%)
  between operations  0.66 us (1%)
    pallas_call x1, Pallas kernels, on_device(): pl.pallas_call(kernel, out_shape=jax.ShapeDtypeStruct(grid.shape, grid.dt...  42.1 us
    unnamed x1, local copies, waits for them, and re-layouts  3.22 us

profile of v2, /device:TPU:0, one launch (start us, length us, event | category | flops | bytes accessed | tf_op | source)
XLA Modules:
  0.0 46.0 jit_solution(4754223711168666004)
XLA Ops:
  0.7 42.1 %shard_map.73 = bf16[64,2,32,256]{3,2,1,0:T(8,128)(2,1)} custom-call(bf16[64,2,32,256]{3,2,1,0:T(8,128)(2,1)} %grid_hbm.1, bf16[9,8,64]{2,1,0:T(8,128)(2,1)} %bitcast.3, f32[1,64]{1,0:T(1,128)} %bitcast.5, f32[3,4,64]{2,1,0:T(4,128)} %bitcast.4, bf16[4,64,64]{2,1,0:T(8,128)(2,1)} %point_hbm.1, s32[1,32]{1,0:T(1,128)} %occupied_hbm.1, s32[1]{0:T(128)S(6)} %copy.9.count_hbm), custom_call_target="tpu_custom_call" | custom-call | flops 4000000000 | bytes 4194304 | tf_op jit(solution)/shard_map/pallas_call | solution.py:317
  42.7 3.2 %copy.10 = bf16[64,2,32,256]{3,2,1,0:T(8,128)(2,1)} copy(bf16[64,2,32,256]{3,2,1,0:T(8,128)(2,1)} %shard_map.73) | data formatting | bytes 4194304

commit v3 on v2

--- a/solution.py
+++ b/solution.py
@@ -40,11 +40,11 @@
 
 def kernel(
     grid_hbm, weight_hbm, bias_hbm, depth_hbm, point_hbm, occupied_hbm, count_hbm,
-    out_ref,
+    hidden_hbm, returned, place_hbm, covered_hbm,
     weight_ref, bias_ref, depth_ref, point_ref, occupied_ref, count_ref, cells, wide, lanes, band,
     slot_band, pick, place, covered, mix, taps, bias_col, row_col, half_col,
-    edge_out, edge_in, hidden, outgoing, incoming, state, answer, returned,
-    load_sems, edge_send, edge_recv, send_sems, recv_sems,
+    edge_out, edge_in, hidden, outgoing, incoming, state, answer,
+    load_sems, keep_sems, edge_send, edge_recv, send_sems, recv_sems,
 ):
     me = lax.axis_index("frame")
     tile = lax.axis_index("tile")
@@ -233,6 +233,17 @@
                 half = act[o * 32 : (o + 1) * 32] + bias_col[pl.ds(8 * g + o, 1), :]
                 value = cells[8 * g + o, f].astype(F32) + gated(half)
                 hidden[8 * g + o, f] = value.astype(BF16)
+
+    kept = []
+
+    def keep(source, target):
+        copy = pltpu.make_async_copy(source, target, keep_sems.at[len(kept)])
+        copy.start()
+        kept.append(copy)
+
+    keep(hidden, hidden_hbm)
+    keep(place, place_hbm)
+    keep(covered, covered_hbm)
 
     def temporal(s):
         state[0:16] = jnp.zeros((16, 64, 128), F32)
@@ -265,14 +276,37 @@
         whole(s, incoming.at[s, pl.ds(0, 15)]).wait_recv()
         temporal(s)
         send(2 + s, lambda to, s=s: answer.at[s, to], returned.at[16 * s + me])
-        returned[16 * s + me] = answer[s, me]
+        keep(answer.at[s, me], returned.at[16 * s + me])
 
     for s in range(2):
         whole(2 + s, returned.at[pl.ds(0, 15)]).wait_recv()
 
-    @pl.loop(0, 4, unroll=2)
-    def _(pair):
-        split = [returned[:, f, pl.ds(16 * pair, 16), :].astype(F32) for f in range(2)]
+    for copy in kept:
+        copy.wait()
+    for s in range(2):
+        whole(s, outgoing.at[pl.ds(0, 15)]).wait_send()
+        whole(2 + s, answer.at[s, pl.ds(0, 15)]).wait_send()
+
+
+def merge(hidden_hbm, returned_hbm, place_hbm, covered_hbm, out_hbm, hidden, returned, place, covered, out, in_sems, out_sems):
+    loads = [
+        pltpu.make_async_copy(place_hbm, place, in_sems.at[8]),
+        pltpu.make_async_copy(covered_hbm, covered, in_sems.at[9]),
+    ]
+    for pair in range(4):
+        span = pl.ds(16 * pair, 16)
+        source, target = returned_hbm.at[:, :, span], returned.at[:, :, span]
+        loads.append(pltpu.make_async_copy(source, target, in_sems.at[2 * pair]))
+        loads.append(pltpu.make_async_copy(hidden_hbm.at[span], hidden.at[span], in_sems.at[2 * pair + 1]))
+    for load in loads:
+        load.start()
+    loads[0].wait()
+    loads[1].wait()
+    stores = []
+    for pair in range(4):
+        loads[2 + 2 * pair].wait()
+        loads[3 + 2 * pair].wait()
+        split = [returned[:, f, 16 * pair : 16 * pair + 16, :].astype(F32) for f in range(2)]
         for e in range(2):
             g = 2 * pair + e
             both = [part[:, 8 * e : 8 * e + 8].reshape(256, 128) for part in split]
@@ -281,13 +315,14 @@
                 for h in range(2):
                     span = slice(128 * h, 128 * h + 128)
                     new = value[256 * h : 256 * h + 256, 128 * f : 128 * f + 128]
-                    old = hidden[pl.ds(8 * g, 8), f, :, span].reshape(256, 128).astype(F32)
+                    old = hidden[8 * g : 8 * g + 8, f, :, span].reshape(256, 128).astype(F32)
                     new = jnp.where(covered[:, span] > 0.5, new, old)
-                    out_ref[pl.ds(8 * g, 8), f, :, span] = new.reshape(8, 32, 128).astype(BF16)
-
-    for s in range(2):
-        whole(s, outgoing.at[pl.ds(0, 15)]).wait_send()
-        whole(2 + s, answer.at[s, pl.ds(0, 15)]).wait_send()
+                    out[8 * g : 8 * g + 8, f, :, span] = new.reshape(8, 32, 128).astype(BF16)
+        span = pl.ds(16 * pair, 16)
+        stores.append(pltpu.make_async_copy(out.at[span], out_hbm.at[span], out_sems.at[pair]))
+        stores[pair].start()
+    for store in stores:
+        store.wait()
 
 
 def on_device(grid, conv_weight, conv_bias, depth_kernel, point_weight, occupied, counts):
@@ -312,13 +347,14 @@
         ((2, 16, 2, 64, 128), BF16),
         ((48, 64, 128), F32),
         ((2, 16, 2, 64, 128), BF16),
-        ((32, 2, 64, 128), BF16),
     ]
-    return pl.pallas_call(
+    kinds = [(grid.shape, BF16), ((32, 2, 64, 128), BF16), ((512, 256), BF16), ((256, 256), F32)]
+    anywhere = pl.BlockSpec(memory_space=pl.ANY)
+    parts = pl.pallas_call(
         kernel,
-        out_shape=jax.ShapeDtypeStruct(grid.shape, grid.dtype),
+        out_shape=[jax.ShapeDtypeStruct(shape, kind) for shape, kind in kinds],
         in_specs=[pl.BlockSpec(memory_space=pltpu.HBM)] * 7,
-        out_specs=pl.BlockSpec(memory_space=pltpu.VMEM),
+        out_specs=[anywhere] * 4,
         scratch_shapes=[
             pltpu.VMEM((9, 8, 64), BF16),
             pltpu.VMEM((1, 64), F32),
@@ -330,6 +366,7 @@
         + [pltpu.VMEM(shape, kind) for shape, kind in buffers]
         + [
             pltpu.SemaphoreType.DMA((7,)),
+            pltpu.SemaphoreType.DMA((5,)),
             pltpu.SemaphoreType.DMA((2,)),
             pltpu.SemaphoreType.DMA((2,)),
             pltpu.SemaphoreType.DMA((4,)),
@@ -348,6 +385,19 @@
         occupied,
         counts,
     )
+    return pl.pallas_call(
+        merge,
+        out_shape=jax.ShapeDtypeStruct(grid.shape, grid.dtype),
+        in_specs=[anywhere] * 4,
+        out_specs=anywhere,
+        scratch_shapes=[pltpu.VMEM(shape, kind) for shape, kind in kinds]
+        + [
+            pltpu.VMEM(grid.shape, BF16),
+            pltpu.SemaphoreType.DMA((10,)),
+            pltpu.SemaphoreType.DMA((4,)),
+        ],
+        compiler_params=pltpu.CompilerParams(vmem_limit_bytes=56 * 1024 * 1024),
+    )(*parts)
 
 
 def solution(mesh):

time: 46.3 us -> 44.4 us (0.959)
  local copies, waits for them, and re-layouts: 3.22 us -> 0 us
  Pallas kernels: 42.1 us -> 43.4 us
    unnamed x1 -> x0, local copies, waits for them, and re-layouts: 3.22 us -> none
    pallas_call x1 -> x2, Pallas kernels: 42.1 us -> 43.4 us  [the longest x1 40 us: on_device(): pl.pallas_call(kernel, out_shape=[jax.ShapeDtypeStruct(shape, kind) for s...]
where the time goes in v3:
time: 44.4 us; the launch traced here: 44 us
  Pallas kernels  43.4 us (98%)
  between operations  0.66 us (1%)
    pallas_call x1, Pallas kernels, on_device(): pl.pallas_call(kernel, out_shape=[jax.ShapeDtypeStruct(shape, kind) for s...  40 us
    pallas_call x1, Pallas kernels, on_device(): pl.pallas_call(merge, out_shape=jax.ShapeDtypeStruct(grid.shape, grid.dty...  3.4 us

profile of v3, /device:TPU:0, one launch (start us, length us, event | category | flops | bytes accessed | tf_op | source)
XLA Modules:
  0.0 44.0 jit_solution(6447608500698750388)
XLA Ops:
  0.7 40.0 %shard_map.73 = (bf16[64,2,32,256]{3,2,1,0:T(8,128)(2,1)}, bf16[32,2,64,128]{3,2,1,0:T(8,128)(2,1)}, bf16[512,256]{1,0:T(8,128)(2,1)}, f32[256,256]{1,0:T(8,128)}) custom-call(bf16[64,2,32,256]{3,2,1,0:T(8,128)(2,1)} %grid_hbm.1, bf16[9,8,64]{2,1,0:T(8,128)(2,1)} %bitcast.3, f32[1,64]{1,0:T(1,128)} %bitcast.5, f32[3,4,64]{2,1,0:T(4,128)} %bitcast.4, ...), custom_call_target="tpu_custom_call" | custom-call | flops 4000000000 | bytes 4194304 | tf_op jit(solution)/shard_map/pallas_call | solution.py:353
  40.6 3.4 %shard_map.74 = bf16[64,2,32,256]{3,2,1,0:T(8,128)(2,1)} custom-call(bf16[64,2,32,256]{3,2,1,0:T(8,128)(2,1)} %get-tuple-element.9.hidden_hbm, bf16[32,2,64,128]{3,2,1,0:T(8,128)(2,1)} %get-tuple-element.10.returned_hbm, bf16[512,256]{1,0:T(8,128)(2,1)} %get-tuple-element.11.place_hbm, f32[256,256]{1,0:T(8,128)} %get-tuple-element.12.covered_hbm), custom_call_target="tpu_custom_call" | custom-call | tf_op jit(solution)/shard_map/pallas_call | solution.py:388

commit v4 on v3

--- a/solution.py
+++ b/solution.py
@@ -44,7 +44,7 @@
     weight_ref, bias_ref, depth_ref, point_ref, occupied_ref, count_ref, cells, wide, lanes, band,
     slot_band, pick, place, covered, mix, taps, bias_col, row_col, half_col,
     edge_out, edge_in, hidden, outgoing, incoming, state, answer,
-    load_sems, keep_sems, edge_send, edge_recv, send_sems, recv_sems,
+    load_sems, keep_sems, edge_send, edge_recv, send_sems, recv_sems, row_sem,
 ):
     me = lax.axis_index("frame")
     tile = lax.axis_index("tile")
@@ -57,8 +57,9 @@
     barrier = pltpu.get_barrier_semaphore()
     for neighbour in (right, left):
         pl.semaphore_signal(barrier, inc=1, device_id=neighbour, device_id_type=MESH)
-    for hop in HOPS:
-        pl.semaphore_signal(barrier, inc=1, device_id={"frame": peer(hop)}, device_id_type=MESH)
+    for d in (2, 1, 3):
+        for hop in ((d, 0), (0, d)):
+            pl.semaphore_signal(barrier, inc=1, device_id={"frame": peer(hop)}, device_id_type=MESH)
     sources = (grid_hbm, weight_hbm, bias_hbm, depth_hbm, point_hbm, occupied_hbm, count_hbm)
     targets = (cells, weight_ref, bias_ref, depth_ref, point_ref, occupied_ref, count_ref)
     loads = []
@@ -70,15 +71,38 @@
     lane, lane_wide = cols((256, 128)), cols((256, 256))
     nought = jnp.zeros((256, 256), BF16)
 
-    def shift(n, edge):
+    def ends(n, edge):
+        block = cells[pl.ds(8 * (n // 2), 8), n % 2].reshape(256, 256)
+        edge = jnp.where(lane == n, pltpu.roll(block[:, 128:], n + 1, 1), edge)
+        return jnp.where(lane == 16 + n, pltpu.roll(block[:, :128], 16 + n, 1), edge)
+
+    edge_out[...] = lax.fori_loop(0, 16, ends, nought[:, :128], unroll=UNROLL)
+
+    pl.semaphore_wait(barrier, 8)
+    edge_copies = []
+    for side, neighbour in enumerate((right, left)):
+        copy = pltpu.make_async_remote_copy(
+            src_ref=edge_out,
+            dst_ref=edge_in.at[side],
+            send_sem=edge_send.at[side],
+            recv_sem=edge_recv.at[side],
+            device_id=neighbour,
+            device_id_type=MESH,
+        )
+        copy.start()
+        edge_copies.append(copy)
+
+    for d in (2, 1, 3):
+        pl.semaphore_signal(row_sem, inc=1, device_id={"frame": peer((0, d))}, device_id_type=MESH)
+
+    def shift(n, carry):
         block = cells[pl.ds(8 * (n // 2), 8), n % 2].reshape(256, 256)
         wide[n, 256:512] = block
         wide[n, 0:256] = jnp.where(lane_wide == 0, nought, pltpu.roll(block, 1, 1))
         wide[n, 512:768] = jnp.where(lane_wide == 255, nought, pltpu.roll(block, 255, 1))
-        edge = jnp.where(lane == n, pltpu.roll(block[:, 128:], n + 1, 1), edge)
-        return jnp.where(lane == 16 + n, pltpu.roll(block[:, :128], 16 + n, 1), edge)
-
-    edge_out[...] = lax.fori_loop(0, 16, shift, nought[:, :128], unroll=UNROLL)
+        return carry
+
+    lax.fori_loop(0, 16, shift, 0, unroll=UNROLL)
 
     for load in loads[1:]:
         load.wait()
@@ -114,53 +138,6 @@
                     parts.append(value)
                 both = jnp.concatenate(parts, axis=0).astype(BF16)
                 slot_band[g, pl.ds(start, 16), dc * 256 : (dc + 1) * 256] = both
-
-    pl.semaphore_wait(barrier, 17)
-    edge_copies = []
-    for side, neighbour in enumerate((right, left)):
-        copy = pltpu.make_async_remote_copy(
-            src_ref=edge_out,
-            dst_ref=edge_in.at[side],
-            send_sem=edge_send.at[side],
-            recv_sem=edge_recv.at[side],
-            device_id=neighbour,
-            device_id_type=MESH,
-        )
-        copy.start()
-        edge_copies.append(copy)
-
-    offset = (cols((32, 256)) & 31) - rows((32, 256))
-
-    @pl.loop(0, 8)
-    def _(g):
-        for dc in range(3):
-            for o in range(8):
-                value = jnp.zeros((32, 256), F32)
-                for dr in range(3):
-                    line = lanes[3 * dr + dc, pl.ds(8 * g + o, 1), :]
-                    value = jnp.where(offset == dr - 1, line, value)
-                band[g, o * 32 : (o + 1) * 32, dc * 256 : (dc + 1) * 256] = value.astype(BF16)
-
-    expand = one_hot((cols((32, 256)) >> 3) == rows((32, 256)))
-    row_lane = dot(jnp.broadcast_to(row_of, (8, 32)).astype(BF16), expand)[0:1]
-    half_lane = dot(jnp.broadcast_to(half_of, (8, 32)).astype(BF16), expand)[0:1]
-    live = (c2 >> 3) < count_ref[0]
-    target = ((r2 >> 5) == (c2 & 7)) & ((r2 & 31).astype(F32) == row_lane) & live
-    for h in range(2):
-        chosen = jnp.where(target & (half_lane == float(h)), 1.0, 0.0)
-        place[h * 256 : (h + 1) * 256, :] = chosen.astype(BF16)
-        covered[:, h * 128 : (h + 1) * 128] = jnp.broadcast_to(jnp.sum(chosen, axis=1, keepdims=True), (256, 128))
-
-    for layer in range(4):
-        for j in range(3):
-            line = 0.5 * depth_ref[j, layer : layer + 1, :]
-            column = jnp.sum(jnp.where(diagonal, line, 0.0), axis=1, keepdims=True)
-            taps[3 * layer + j] = jnp.broadcast_to(column, (64, 128))
-    repeat = one_hot((rows((256, 64)) & 63) == cols((256, 64)))
-    for layer in range(4):
-        tall = dot(repeat, point_ref[layer]).astype(BF16)
-        full = dot(tall, repeat, ((1,), (1,)))
-        mix[layer] = jnp.where((r2 >> 6) == (c2 >> 6), full, 0.0).astype(BF16)
 
     for copy in edge_copies:
         copy.wait()
@@ -222,8 +199,45 @@
 
     for s in range(2):
         slots(s)
+        if s == 0:
+            pl.semaphore_wait(row_sem, 3)
+        else:
+            whole(0, outgoing.at[pl.ds(0, 15)]).wait_send()
         send(s, lambda to, s=s: outgoing.at[16 * s + to], incoming.at[s, me])
         incoming[s, me] = outgoing[16 * s + me]
+
+    offset = (cols((32, 256)) & 31) - rows((32, 256))
+
+    @pl.loop(0, 8)
+    def _(g):
+        for dc in range(3):
+            for o in range(8):
+                value = jnp.zeros((32, 256), F32)
+                for dr in range(3):
+                    line = lanes[3 * dr + dc, pl.ds(8 * g + o, 1), :]
+                    value = jnp.where(offset == dr - 1, line, value)
+                band[g, o * 32 : (o + 1) * 32, dc * 256 : (dc + 1) * 256] = value.astype(BF16)
+
+    expand = one_hot((cols((32, 256)) >> 3) == rows((32, 256)))
+    row_lane = dot(jnp.broadcast_to(row_of, (8, 32)).astype(BF16), expand)[0:1]
+    half_lane = dot(jnp.broadcast_to(half_of, (8, 32)).astype(BF16), expand)[0:1]
+    live = (c2 >> 3) < count_ref[0]
+    target = ((r2 >> 5) == (c2 & 7)) & ((r2 & 31).astype(F32) == row_lane) & live
+    for h in range(2):
+        chosen = jnp.where(target & (half_lane == float(h)), 1.0, 0.0)
+        place[h * 256 : (h + 1) * 256, :] = chosen.astype(BF16)
+        covered[:, h * 128 : (h + 1) * 128] = jnp.broadcast_to(jnp.sum(chosen, axis=1, keepdims=True), (256, 128))
+
+    for layer in range(4):
+        for j in range(3):
+            line = 0.5 * depth_ref[j, layer : layer + 1, :]
+            column = jnp.sum(jnp.where(diagonal, line, 0.0), axis=1, keepdims=True)
+            taps[3 * layer + j] = jnp.broadcast_to(column, (64, 128))
+    repeat = one_hot((rows((256, 64)) & 63) == cols((256, 64)))
+    for layer in range(4):
+        tall = dot(repeat, point_ref[layer]).astype(BF16)
+        full = dot(tall, repeat, ((1,), (1,)))
+        mix[layer] = jnp.where((r2 >> 6) == (c2 >> 6), full, 0.0).astype(BF16)
 
     @pl.loop(0, 8, unroll=2)
     def _(g):
@@ -284,7 +298,8 @@
     for copy in kept:
         copy.wait()
     for s in range(2):
-        whole(s, outgoing.at[pl.ds(0, 15)]).wait_send()
+        if s:
+            whole(s, outgoing.at[pl.ds(0, 15)]).wait_send()
         whole(2 + s, answer.at[s, pl.ds(0, 15)]).wait_send()
 
 
@@ -371,6 +386,7 @@
             pltpu.SemaphoreType.DMA((2,)),
             pltpu.SemaphoreType.DMA((4,)),
             pltpu.SemaphoreType.DMA((4,)),
+            pltpu.SemaphoreType.REGULAR,
         ],
         compiler_params=pltpu.CompilerParams(
             collective_id=0, has_side_effects=True, vmem_limit_bytes=56 * 1024 * 1024

time: 44.4 us -> 41.8 us (0.941)
  Pallas kernels: 43.4 us -> 40.8 us
    pallas_call x1, Pallas kernels: 40 us -> 37.4 us  [on_device(): pl.pallas_call(kernel, out_shape=[jax.ShapeDtypeStruct(shape, kind) for s...]
where the time goes in v4:
time: 41.8 us; the launch traced here: 41.4 us
  Pallas kernels  40.8 us (98%)
  between operations  0.66 us (2%)
    pallas_call x1, Pallas kernels, on_device(): pl.pallas_call(kernel, out_shape=[jax.ShapeDtypeStruct(shape, kind) for s...  37.4 us
    pallas_call x1, Pallas kernels, on_device(): pl.pallas_call(merge, out_shape=jax.ShapeDtypeStruct(grid.shape, grid.dty...  3.4 us

profile of v4, /device:TPU:0, one launch (start us, length us, event | category | flops | bytes accessed | tf_op | source)
XLA Modules:
  0.0 41.4 jit_solution(8458116856351739271)
XLA Ops:
  0.7 37.4 %shard_map.73 = (bf16[64,2,32,256]{3,2,1,0:T(8,128)(2,1)}, bf16[32,2,64,128]{3,2,1,0:T(8,128)(2,1)}, bf16[512,256]{1,0:T(8,128)(2,1)}, f32[256,256]{1,0:T(8,128)}) custom-call(bf16[64,2,32,256]{3,2,1,0:T(8,128)(2,1)} %grid_hbm.1, bf16[9,8,64]{2,1,0:T(8,128)(2,1)} %bitcast.3, f32[1,64]{1,0:T(1,128)} %bitcast.5, f32[3,4,64]{2,1,0:T(4,128)} %bitcast.4, ...), custom_call_target="tpu_custom_call" | custom-call | flops 4000000000 | bytes 4194304 | tf_op jit(solution)/shard_map/pallas_call | solution.py:368
  38.0 3.4 %shard_map.74 = bf16[64,2,32,256]{3,2,1,0:T(8,128)(2,1)} custom-call(bf16[64,2,32,256]{3,2,1,0:T(8,128)(2,1)} %get-tuple-element.9.hidden_hbm, bf16[32,2,64,128]{3,2,1,0:T(8,128)(2,1)} %get-tuple-element.10.returned_hbm, bf16[512,256]{1,0:T(8,128)(2,1)} %get-tuple-element.11.place_hbm, f32[256,256]{1,0:T(8,128)} %get-tuple-element.12.covered_hbm), custom_call_target="tpu_custom_call" | custom-call | tf_op jit(solution)/shard_map/pallas_call | solution.py:404

commit v5 on v4

--- a/solution.py
+++ b/solution.py
@@ -40,11 +40,11 @@
 
 def kernel(
     grid_hbm, weight_hbm, bias_hbm, depth_hbm, point_hbm, occupied_hbm, count_hbm,
-    hidden_hbm, returned, place_hbm, covered_hbm,
+    out_ref,
     weight_ref, bias_ref, depth_ref, point_ref, occupied_ref, count_ref, cells, wide, lanes, band,
     slot_band, pick, place, covered, mix, taps, bias_col, row_col, half_col,
-    edge_out, edge_in, hidden, outgoing, incoming, state, answer,
-    load_sems, keep_sems, edge_send, edge_recv, send_sems, recv_sems, row_sem,
+    edge_out, edge_in, outgoing, incoming, state, answer, returned,
+    load_sems, edge_send, edge_recv, send_sems, recv_sems, row_sem,
 ):
     me = lax.axis_index("frame")
     tile = lax.axis_index("tile")
@@ -226,7 +226,9 @@
     for h in range(2):
         chosen = jnp.where(target & (half_lane == float(h)), 1.0, 0.0)
         place[h * 256 : (h + 1) * 256, :] = chosen.astype(BF16)
-        covered[:, h * 128 : (h + 1) * 128] = jnp.broadcast_to(jnp.sum(chosen, axis=1, keepdims=True), (256, 128))
+        for s in range(2):
+            found = jnp.sum(chosen[:, 128 * s : 128 * s + 128], axis=1, keepdims=True)
+            covered[s, :, h * 128 : (h + 1) * 128] = jnp.broadcast_to(found, (256, 128))
 
     for layer in range(4):
         for j in range(3):
@@ -246,18 +248,7 @@
             for o in range(8):
                 half = act[o * 32 : (o + 1) * 32] + bias_col[pl.ds(8 * g + o, 1), :]
                 value = cells[8 * g + o, f].astype(F32) + gated(half)
-                hidden[8 * g + o, f] = value.astype(BF16)
-
-    kept = []
-
-    def keep(source, target):
-        copy = pltpu.make_async_copy(source, target, keep_sems.at[len(kept)])
-        copy.start()
-        kept.append(copy)
-
-    keep(hidden, hidden_hbm)
-    keep(place, place_hbm)
-    keep(covered, covered_hbm)
+                out_ref[8 * g + o, f] = value.astype(BF16)
 
     def temporal(s):
         state[0:16] = jnp.zeros((16, 64, 128), F32)
@@ -290,54 +281,32 @@
         whole(s, incoming.at[s, pl.ds(0, 15)]).wait_recv()
         temporal(s)
         send(2 + s, lambda to, s=s: answer.at[s, to], returned.at[16 * s + me])
-        keep(answer.at[s, me], returned.at[16 * s + me])
+        returned[16 * s + me] = answer[s, me]
+
+    def merge(s):
+        @pl.loop(0, 4, unroll=2)
+        def _(pair):
+            split = [returned[16 * s : 16 * s + 16, f, pl.ds(16 * pair, 16), :].astype(F32) for f in range(2)]
+            for e in range(2):
+                g = 2 * pair + e
+                both = [part[:, 8 * e : 8 * e + 8].reshape(128, 128) for part in split]
+                value = dot(place[:, 128 * s : 128 * s + 128], jnp.concatenate(both, axis=1).astype(BF16))
+                for f in range(2):
+                    for h in range(2):
+                        span = slice(128 * h, 128 * h + 128)
+                        new = value[256 * h : 256 * h + 256, 128 * f : 128 * f + 128]
+                        old = out_ref[pl.ds(8 * g, 8), f, :, span].reshape(256, 128).astype(F32)
+                        new = jnp.where(covered[s, :, span] > 0.5, new, old)
+                        out_ref[pl.ds(8 * g, 8), f, :, span] = new.reshape(8, 32, 128).astype(BF16)
 
     for s in range(2):
         whole(2 + s, returned.at[pl.ds(0, 15)]).wait_recv()
-
-    for copy in kept:
-        copy.wait()
+        merge(s)
+
     for s in range(2):
         if s:
             whole(s, outgoing.at[pl.ds(0, 15)]).wait_send()
         whole(2 + s, answer.at[s, pl.ds(0, 15)]).wait_send()
-
-
-def merge(hidden_hbm, returned_hbm, place_hbm, covered_hbm, out_hbm, hidden, returned, place, covered, out, in_sems, out_sems):
-    loads = [
-        pltpu.make_async_copy(place_hbm, place, in_sems.at[8]),
-        pltpu.make_async_copy(covered_hbm, covered, in_sems.at[9]),
-    ]
-    for pair in range(4):
-        span = pl.ds(16 * pair, 16)
-        source, target = returned_hbm.at[:, :, span], returned.at[:, :, span]
-        loads.append(pltpu.make_async_copy(source, target, in_sems.at[2 * pair]))
-        loads.append(pltpu.make_async_copy(hidden_hbm.at[span], hidden.at[span], in_sems.at[2 * pair + 1]))
-    for load in loads:
-        load.start()
-    loads[0].wait()
-    loads[1].wait()
-    stores = []
-    for pair in range(4):
-        loads[2 + 2 * pair].wait()
-        loads[3 + 2 * pair].wait()
-        split = [returned[:, f, 16 * pair : 16 * pair + 16, :].astype(F32) for f in range(2)]
-        for e in range(2):
-            g = 2 * pair + e
-            both = [part[:, 8 * e : 8 * e + 8].reshape(256, 128) for part in split]
-            value = dot(place[...], jnp.concatenate(both, axis=1).astype(BF16))
-            for f in range(2):
-                for h in range(2):
-                    span = slice(128 * h, 128 * h + 128)
-                    new = value[256 * h : 256 * h + 256, 128 * f : 128 * f + 128]
-                    old = hidden[8 * g : 8 * g + 8, f, :, span].reshape(256, 128).astype(F32)
-                    new = jnp.where(covered[:, span] > 0.5, new, old)
-                    out[8 * g : 8 * g + 8, f, :, span] = new.reshape(8, 32, 128).astype(BF16)
-        span = pl.ds(16 * pair, 16)
-        stores.append(pltpu.make_async_copy(out.at[span], out_hbm.at[span], out_sems.at[pair]))
-        stores[pair].start()
-    for store in stores:
-        store.wait()
 
 
 def on_device(grid, conv_weight, conv_bias, depth_kernel, point_weight, occupied, counts):
@@ -349,7 +318,7 @@
         ((8, 256, 768), BF16),
         ((256, 256), BF16),
         ((512, 256), BF16),
-        ((256, 256), F32),
+        ((2, 256, 256), F32),
         ((4, 256, 256), BF16),
         ((12, 64, 128), F32),
         ((64, 256), F32),
@@ -357,19 +326,17 @@
         ((256, 128), F32),
         ((256, 128), BF16),
         ((2, 256, 128), BF16),
-        ((64, 2, 32, 256), BF16),
         ((32, 2, 64, 128), BF16),
         ((2, 16, 2, 64, 128), BF16),
         ((48, 64, 128), F32),
         ((2, 16, 2, 64, 128), BF16),
+        ((32, 2, 64, 128), BF16),
     ]
-    kinds = [(grid.shape, BF16), ((32, 2, 64, 128), BF16), ((512, 256), BF16), ((256, 256), F32)]
-    anywhere = pl.BlockSpec(memory_space=pl.ANY)
-    parts = pl.pallas_call(
+    return pl.pallas_call(
         kernel,
-        out_shape=[jax.ShapeDtypeStruct(shape, kind) for shape, kind in kinds],
+        out_shape=jax.ShapeDtypeStruct(grid.shape, grid.dtype),
         in_specs=[pl.BlockSpec(memory_space=pltpu.HBM)] * 7,
-        out_specs=[anywhere] * 4,
+        out_specs=pl.BlockSpec(memory_space=pltpu.VMEM),
         scratch_shapes=[
             pltpu.VMEM((9, 8, 64), BF16),
             pltpu.VMEM((1, 64), F32),
@@ -381,7 +348,6 @@
         + [pltpu.VMEM(shape, kind) for shape, kind in buffers]
         + [
             pltpu.SemaphoreType.DMA((7,)),
-            pltpu.SemaphoreType.DMA((5,)),
             pltpu.SemaphoreType.DMA((2,)),
             pltpu.SemaphoreType.DMA((2,)),
             pltpu.SemaphoreType.DMA((4,)),
@@ -389,31 +355,23 @@
             pltpu.SemaphoreType.REGULAR,
         ],
         compiler_params=pltpu.CompilerParams(
-            collective_id=0, has_side_effects=True, vmem_limit_bytes=56 * 1024 * 1024
+            collective_id=0, has_side_effects=True, vmem_limit_bytes=36 * 1024 * 1024
         ),
-        cost_estimate=pl.CostEstimate(flops=4_000_000_000, bytes_accessed=4 << 20, transcendentals=3 << 20),
+        cost_estimate=pl.CostEstimate(flops=4_000_000_000, bytes_accessed=0, transcendentals=3 << 20),
     )(
-        grid,
-        conv_weight.transpose(0, 2, 1),
-        conv_bias.reshape(1, 64),
-        depth_kernel.transpose(1, 0, 2),
-        point_weight,
-        occupied,
+        *(
+            pltpu.with_memory_space_constraint(array, pltpu.HBM)
+            for array in (
+                grid,
+                conv_weight.transpose(0, 2, 1),
+                conv_bias.reshape(1, 64),
+                depth_kernel.transpose(1, 0, 2),
+                point_weight,
+                occupied,
+            )
+        ),
         counts,
     )
-    return pl.pallas_call(
-        merge,
-        out_shape=jax.ShapeDtypeStruct(grid.shape, grid.dtype),
-        in_specs=[anywhere] * 4,
-        out_specs=anywhere,
-        scratch_shapes=[pltpu.VMEM(shape, kind) for shape, kind in kinds]
-        + [
-            pltpu.VMEM(grid.shape, BF16),
-            pltpu.SemaphoreType.DMA((10,)),
-            pltpu.SemaphoreType.DMA((4,)),
-        ],
-        compiler_params=pltpu.CompilerParams(vmem_limit_bytes=56 * 1024 * 1024),
-    )(*parts)
 
 
 def solution(mesh):

time: 41.8 us -> 40.4 us (0.967)
  Pallas kernels: 40.8 us -> 38.1 us
  local copies, waits for them, and re-layouts: 0 us -> 1.32 us
    pallas_call x2 -> x1, Pallas kernels: 40.8 us -> 38.1 us  [on_device(): pl.pallas_call(kernel, out_shape=jax.ShapeDtypeStruct(grid.shape, grid.dt...]
    unnamed x0 -> x1, local copies, waits for them, and re-layouts: none -> 1.32 us
where the time goes in v5:
time: 40.4 us; the launch traced here: 40 us
  Pallas kernels  38.1 us (94%)
  local copies, waits for them, and re-layouts  1.32 us (3%)
  between operations  0.66 us (2%)
    pallas_call x1, Pallas kernels, on_device(): pl.pallas_call(kernel, out_shape=jax.ShapeDtypeStruct(grid.shape, grid.dt...  38.1 us
    unnamed x1, local copies, waits for them, and re-layouts  1.32 us

profile of v5, /device:TPU:0, one launch (start us, length us, event | category | flops | bytes accessed | tf_op | source)
XLA Modules:
  0.0 40.0 jit_solution(6305058461204597261)
XLA Ops:
  0.7 38.1 %shard_map.73 = bf16[64,2,32,256]{3,2,1,0:T(8,128)(2,1)S(1)} custom-call(bf16[64,2,32,256]{3,2,1,0:T(8,128)(2,1)} %grid_hbm.1, bf16[9,8,64]{2,1,0:T(8,128)(2,1)} %bitcast.3, f32[1,64]{1,0:T(1,128)} %bitcast.5, f32[3,4,64]{2,1,0:T(4,128)} %bitcast.4, bf16[4,64,64]{2,1,0:T(8,128)(2,1)} %point_hbm.1, s32[1,32]{1,0:T(1,128)} %occupied_hbm.1, s32[1]{0:T(128)S(6)} %copy.9.count_hbm), custom_call_target="tpu_custom_call" | custom-call | flops 4000000000 | tf_op jit(solution)/shard_map/pallas_call | solution.py:335
  38.7 1.3 %copy.10 = bf16[64,2,32,256]{3,2,1,0:T(8,128)(2,1)} copy(bf16[64,2,32,256]{3,2,1,0:T(8,128)(2,1)S(1)} %shard_map.73) | data formatting | bytes 4194304

commit v6 on v5

--- a/solution.py
+++ b/solution.py
@@ -10,7 +10,7 @@
 MESH = pl.DeviceIdType.MESH
 F32 = jnp.float32
 BF16 = jnp.bfloat16
-UNROLL = 4
+UNROLL = 16
 
 HOPS = (
     (2, 2), (2, 1), (2, 3), (1, 2), (3, 2), (2, 0), (0, 2),
@@ -60,14 +60,18 @@
     for d in (2, 1, 3):
         for hop in ((d, 0), (0, d)):
             pl.semaphore_signal(barrier, inc=1, device_id={"frame": peer(hop)}, device_id_type=MESH)
-    sources = (grid_hbm, weight_hbm, bias_hbm, depth_hbm, point_hbm, occupied_hbm, count_hbm)
-    targets = (cells, weight_ref, bias_ref, depth_ref, point_ref, occupied_ref, count_ref)
+    sources = (weight_hbm, bias_hbm, depth_hbm, point_hbm, occupied_hbm, count_hbm)
+    targets = (weight_ref, bias_ref, depth_ref, point_ref, occupied_ref, count_ref)
+    quarters = []
+    for i in range(4):
+        span = pl.ds(16 * i, 16)
+        quarters.append(pltpu.make_async_copy(grid_hbm.at[span], cells.at[span], load_sems.at[7 + i]))
+        quarters[i].start()
     loads = []
     for i, (source, target) in enumerate(zip(sources, targets)):
         loads.append(pltpu.make_async_copy(source, target, load_sems.at[i]))
         loads[i].start()
 
-    loads[0].wait()
     lane, lane_wide = cols((256, 128)), cols((256, 256))
     nought = jnp.zeros((256, 256), BF16)
 
@@ -76,7 +80,11 @@
         edge = jnp.where(lane == n, pltpu.roll(block[:, 128:], n + 1, 1), edge)
         return jnp.where(lane == 16 + n, pltpu.roll(block[:, :128], 16 + n, 1), edge)
 
-    edge_out[...] = lax.fori_loop(0, 16, ends, nought[:, :128], unroll=UNROLL)
+    edge = nought[:, :128]
+    for i in range(4):
+        quarters[i].wait()
+        edge = lax.fori_loop(4 * i, 4 * i + 4, ends, edge, unroll=4)
+    edge_out[...] = edge
 
     pl.semaphore_wait(barrier, 8)
     edge_copies = []
@@ -104,7 +112,7 @@
 
     lax.fori_loop(0, 16, shift, 0, unroll=UNROLL)
 
-    for load in loads[1:]:
+    for load in loads:
         load.wait()
     r2, c2 = rows((256, 256)), cols((256, 256))
     listed = occupied_ref[...]
@@ -156,7 +164,7 @@
     def slots(s):
         lo = 128 * s
 
-        @pl.loop(0, 4, unroll=2)
+        @pl.loop(0, 4, unroll=4)
         def _(pair):
             second = half_col[lo : lo + 128] > 0.5
             for f in range(2):
@@ -347,7 +355,7 @@
         ]
         + [pltpu.VMEM(shape, kind) for shape, kind in buffers]
         + [
-            pltpu.SemaphoreType.DMA((7,)),
+            pltpu.SemaphoreType.DMA((11,)),
             pltpu.SemaphoreType.DMA((2,)),
             pltpu.SemaphoreType.DMA((2,)),
             pltpu.SemaphoreType.DMA((4,)),

time: 40.4 us -> 39 us (0.965)
  Pallas kernels: 38.1 us -> 36.9 us
    pallas_call x1, Pallas kernels: 38.1 us -> 36.9 us  [on_device(): pl.pallas_call(kernel, out_shape=jax.ShapeDtypeStruct(grid.shape, grid.dt...]
where the time goes in v6:
time: 39 us; the launch traced here: 38.9 us
  Pallas kernels  36.9 us (95%)
  local copies, waits for them, and re-layouts  1.32 us (3%)
  between operations  0.66 us (2%)
    pallas_call x1, Pallas kernels, on_device(): pl.pallas_call(kernel, out_shape=jax.ShapeDtypeStruct(grid.shape, grid.dt...  36.9 us
    unnamed x1, local copies, waits for them, and re-layouts  1.32 us

profile of v6, /device:TPU:0, one launch (start us, length us, event | category | flops | bytes accessed | tf_op | source)
XLA Modules:
  0.0 38.9 jit_solution(9339272913671201641)
XLA Ops:
  0.7 36.9 %shard_map.73 = bf16[64,2,32,256]{3,2,1,0:T(8,128)(2,1)S(1)} custom-call(bf16[64,2,32,256]{3,2,1,0:T(8,128)(2,1)} %grid_hbm.1, bf16[9,8,64]{2,1,0:T(8,128)(2,1)} %bitcast.3, f32[1,64]{1,0:T(1,128)} %bitcast.5, f32[3,4,64]{2,1,0:T(4,128)} %bitcast.4, bf16[4,64,64]{2,1,0:T(8,128)(2,1)} %point_hbm.1, s32[1,32]{1,0:T(1,128)} %occupied_hbm.1, s32[1]{0:T(128)S(6)} %copy.9.count_hbm), custom_call_target="tpu_custom_call" | custom-call | flops 4000000000 | tf_op jit(solution)/shard_map/pallas_call | solution.py:343
  37.5 1.3 %copy.10 = bf16[64,2,32,256]{3,2,1,0:T(8,128)(2,1)} copy(bf16[64,2,32,256]{3,2,1,0:T(8,128)(2,1)S(1)} %shard_map.73) | data formatting | bytes 4194304

commit v7 on v6

--- a/solution.py
+++ b/solution.py
@@ -40,10 +40,10 @@
 
 def kernel(
     grid_hbm, weight_hbm, bias_hbm, depth_hbm, point_hbm, occupied_hbm, count_hbm,
-    out_ref,
+    out_ref, returned, place, covered_last,
     weight_ref, bias_ref, depth_ref, point_ref, occupied_ref, count_ref, cells, wide, lanes, band,
-    slot_band, pick, place, covered, mix, taps, bias_col, row_col, half_col,
-    edge_out, edge_in, outgoing, incoming, state, answer, returned,
+    slot_band, pick, covered, mix, taps, bias_col, row_col, half_col,
+    edge_out, edge_in, outgoing, incoming, state, answer,
     load_sems, edge_send, edge_recv, send_sems, recv_sems, row_sem,
 ):
     me = lax.axis_index("frame")
@@ -72,25 +72,28 @@
         loads.append(pltpu.make_async_copy(source, target, load_sems.at[i]))
         loads[i].start()
 
-    lane, lane_wide = cols((256, 128)), cols((256, 256))
+    lane, lane_wide = cols((32, 128)), cols((256, 256))
     nought = jnp.zeros((256, 256), BF16)
 
-    def ends(n, edge):
-        block = cells[pl.ds(8 * (n // 2), 8), n % 2].reshape(256, 256)
-        edge = jnp.where(lane == n, pltpu.roll(block[:, 128:], n + 1, 1), edge)
-        return jnp.where(lane == 16 + n, pltpu.roll(block[:, :128], 16 + n, 1), edge)
-
-    edge = nought[:, :128]
+    def ends(n, edges):
+        block = cells[pl.ds(8 * (n // 2), 8), n % 2]
+        last, first = edges
+        for i in range(8):
+            last = jnp.where(lane == 16 * i + n, pltpu.roll(block[i, :, 128:], (16 * i + n + 1) % 128, 1), last)
+            first = jnp.where(lane == 16 * i + n, pltpu.roll(block[i, :, :128], 16 * i + n, 1), first)
+        return last, first
+
+    edges = (nought[:32, :128], nought[:32, :128])
     for i in range(4):
         quarters[i].wait()
-        edge = lax.fori_loop(4 * i, 4 * i + 4, ends, edge, unroll=4)
-    edge_out[...] = edge
+        edges = lax.fori_loop(4 * i, 4 * i + 4, ends, edges, unroll=4)
+    edge_out[0], edge_out[1] = edges
 
     pl.semaphore_wait(barrier, 8)
     edge_copies = []
     for side, neighbour in enumerate((right, left)):
         copy = pltpu.make_async_remote_copy(
-            src_ref=edge_out,
+            src_ref=edge_out.at[side],
             dst_ref=edge_in.at[side],
             send_sem=edge_send.at[side],
             recv_sem=edge_recv.at[side],
@@ -132,31 +135,36 @@
         lanes[tap] = 0.5 * dot(weight_ref[tap], spread, ((0,), (0,)))
     row_lanes = (cols((8, 256)) & 31).astype(F32)
 
-    @pl.loop(0, 16)
-    def _(pair):
-        start = pl.multiple_of(16 * pair, 16)
-        delta = [row_lanes - row_col[pl.ds(start + 8 * k, 8)] for k in range(2)]
-        for g in range(8):
-            for dc in range(3):
-                parts = []
-                for k in range(2):
-                    value = jnp.zeros((8, 256), F32)
-                    for dr in range(3):
-                        value = jnp.where(delta[k] == dr - 1.0, lanes[3 * dr + dc, 8 * g : 8 * g + 8], value)
-                    parts.append(value)
-                both = jnp.concatenate(parts, axis=0).astype(BF16)
-                slot_band[g, pl.ds(start, 16), dc * 256 : (dc + 1) * 256] = both
-
+    def fill(s):
+        @pl.loop(8 * s, 8 * s + 8)
+        def _(pair):
+            start = pl.multiple_of(16 * pair, 16)
+            delta = [row_lanes - row_col[pl.ds(start + 8 * k, 8)] for k in range(2)]
+            for g in range(8):
+                for dc in range(3):
+                    parts = []
+                    for k in range(2):
+                        value = jnp.zeros((8, 256), F32)
+                        for dr in range(3):
+                            value = jnp.where(delta[k] == dr - 1.0, lanes[3 * dr + dc, 8 * g : 8 * g + 8], value)
+                        parts.append(value)
+                    both = jnp.concatenate(parts, axis=0).astype(BF16)
+                    slot_band[g, pl.ds(start, 16), dc * 256 : (dc + 1) * 256] = both
+
+    fill(0)
     for copy in edge_copies:
         copy.wait()
-    from_left = jnp.where(tile > 0, edge_in[0], nought[:, :128])
-    from_right = jnp.where(tile < 7, edge_in[1], nought[:, :128])
+    from_left = jnp.where(tile > 0, edge_in[0], nought[:32, :128])
+    from_right = jnp.where(tile < 7, edge_in[1], nought[:32, :128])
 
     def fix(n, carry):
-        old = wide[n, 0:256, 0:128]
-        wide[n, 0:256, 0:128] = jnp.where(lane == 0, pltpu.roll(from_left, (128 - n) % 128, 1), old)
-        old = wide[n, 512:768, 128:256]
-        wide[n, 512:768, 128:256] = jnp.where(lane == 127, pltpu.roll(from_right, 111 - n, 1), old)
+        for i in range(8):
+            span = slice(32 * i, 32 * i + 32)
+            edge = pltpu.roll(from_left, (128 - 16 * i - n) % 128, 1)
+            wide[n, span, 0:128] = jnp.where(lane == 0, edge, wide[n, span, 0:128])
+            span = slice(512 + 32 * i, 544 + 32 * i)
+            edge = pltpu.roll(from_right, 127 - 16 * i - n, 1)
+            wide[n, span, 128:256] = jnp.where(lane == 127, edge, wide[n, span, 128:256])
         return carry
 
     lax.fori_loop(0, 16, fix, 0, unroll=UNROLL)
@@ -206,6 +214,8 @@
         )
 
     for s in range(2):
+        if s == 1:
+            fill(1)
         slots(s)
         if s == 0:
             pl.semaphore_wait(row_sem, 3)
@@ -236,7 +246,8 @@
         place[h * 256 : (h + 1) * 256, :] = chosen.astype(BF16)
         for s in range(2):
             found = jnp.sum(chosen[:, 128 * s : 128 * s + 128], axis=1, keepdims=True)
-            covered[s, :, h * 128 : (h + 1) * 128] = jnp.broadcast_to(found, (256, 128))
+            cover = covered if s == 0 else covered_last
+            cover[:, h * 128 : (h + 1) * 128] = jnp.broadcast_to(found, (256, 128))
 
     for layer in range(4):
         for j in range(3):
@@ -291,30 +302,41 @@
         send(2 + s, lambda to, s=s: answer.at[s, to], returned.at[16 * s + me])
         returned[16 * s + me] = answer[s, me]
 
-    def merge(s):
-        @pl.loop(0, 4, unroll=2)
-        def _(pair):
-            split = [returned[16 * s : 16 * s + 16, f, pl.ds(16 * pair, 16), :].astype(F32) for f in range(2)]
-            for e in range(2):
-                g = 2 * pair + e
-                both = [part[:, 8 * e : 8 * e + 8].reshape(128, 128) for part in split]
-                value = dot(place[:, 128 * s : 128 * s + 128], jnp.concatenate(both, axis=1).astype(BF16))
-                for f in range(2):
-                    for h in range(2):
-                        span = slice(128 * h, 128 * h + 128)
-                        new = value[256 * h : 256 * h + 256, 128 * f : 128 * f + 128]
-                        old = out_ref[pl.ds(8 * g, 8), f, :, span].reshape(256, 128).astype(F32)
-                        new = jnp.where(covered[s, :, span] > 0.5, new, old)
-                        out_ref[pl.ds(8 * g, 8), f, :, span] = new.reshape(8, 32, 128).astype(BF16)
-
     for s in range(2):
         whole(2 + s, returned.at[pl.ds(0, 15)]).wait_recv()
-        merge(s)
+        if s == 0:
+            pl.loop(0, 4, unroll=2)(functools.partial(merge, s, out_ref, out_ref, returned, place, covered))
 
     for s in range(2):
         if s:
             whole(s, outgoing.at[pl.ds(0, 15)]).wait_send()
         whole(2 + s, answer.at[s, pl.ds(0, 15)]).wait_send()
+
+
+def merge(s, old_ref, new_ref, returned, place, covered, pair):
+    split = [returned[16 * s : 16 * s + 16, f, pl.ds(16 * pair, 16), :].astype(F32) for f in range(2)]
+    for e in range(2):
+        g = 2 * pair + e
+        both = [part[:, 8 * e : 8 * e + 8].reshape(128, 128) for part in split]
+        value = dot(place[:, 128 * s : 128 * s + 128], jnp.concatenate(both, axis=1).astype(BF16))
+        for f in range(2):
+            for h in range(2):
+                span = slice(128 * h, 128 * h + 128)
+                new = value[256 * h : 256 * h + 256, 128 * f : 128 * f + 128]
+                old = old_ref[pl.ds(8 * g, 8), f, :, span].reshape(256, 128).astype(F32)
+                new = jnp.where(covered[:, span] > 0.5, new, old)
+                new_ref[pl.ds(8 * g, 8), f, :, span] = new.reshape(8, 32, 128).astype(BF16)
+
+
+def finish(old_ref, returned, place, covered, out_hbm, out, sems):
+    copies = []
+    for pair in range(4):
+        merge(1, old_ref, out, returned, place, covered, pair)
+        span = pl.ds(16 * pair, 16)
+        copies.append(pltpu.make_async_copy(out.at[span], out_hbm.at[span], sems.at[pair]))
+        copies[pair].start()
+    for copy in copies:
+        copy.wait()
 
 
 def on_device(grid, conv_weight, conv_bias, depth_kernel, point_weight, occupied, counts):
@@ -325,26 +347,26 @@
         ((8, 256, 768), BF16),
         ((8, 256, 768), BF16),
         ((256, 256), BF16),
-        ((512, 256), BF16),
-        ((2, 256, 256), F32),
+        ((256, 256), F32),
         ((4, 256, 256), BF16),
         ((12, 64, 128), F32),
         ((64, 256), F32),
         ((256, 256), F32),
         ((256, 128), F32),
-        ((256, 128), BF16),
-        ((2, 256, 128), BF16),
+        ((2, 32, 128), BF16),
+        ((2, 32, 128), BF16),
         ((32, 2, 64, 128), BF16),
         ((2, 16, 2, 64, 128), BF16),
         ((48, 64, 128), F32),
         ((2, 16, 2, 64, 128), BF16),
-        ((32, 2, 64, 128), BF16),
     ]
-    return pl.pallas_call(
+    kinds = [(grid.shape, BF16), ((32, 2, 64, 128), BF16), ((512, 256), BF16), ((256, 256), F32)]
+    vmem = pl.BlockSpec(memory_space=pltpu.VMEM)
+    parts = pl.pallas_call(
         kernel,
-        out_shape=jax.ShapeDtypeStruct(grid.shape, grid.dtype),
+        out_shape=[jax.ShapeDtypeStruct(shape, kind) for shape, kind in kinds],
         in_specs=[pl.BlockSpec(memory_space=pltpu.HBM)] * 7,
-        out_specs=pl.BlockSpec(memory_space=pltpu.VMEM),
+        out_specs=[vmem] * 4,
         scratch_shapes=[
             pltpu.VMEM((9, 8, 64), BF16),
             pltpu.VMEM((1, 64), F32),
@@ -380,6 +402,14 @@
         ),
         counts,
     )
+    return pl.pallas_call(
+        finish,
+        out_shape=jax.ShapeDtypeStruct(grid.shape, grid.dtype),
+        in_specs=[vmem] * 4,
+        out_specs=pl.BlockSpec(memory_space=pl.ANY),
+        scratch_shapes=[pltpu.VMEM(grid.shape, BF16), pltpu.SemaphoreType.DMA((4,))],
+        compiler_params=pltpu.CompilerParams(vmem_limit_bytes=36 * 1024 * 1024),
+    )(*parts)
 
 
 def solution(mesh):

time: 39 us -> 37.8 us (0.969)
  local copies, waits for them, and re-layouts: 1.32 us -> 0 us
    unnamed x1 -> x0, local copies, waits for them, and re-layouts: 1.32 us -> none
    pallas_call x1 -> x2, Pallas kernels: 36.9 us -> 37 us  [the longest x1 35.4 us: on_device(): pl.pallas_call(kernel, out_shape=[jax.ShapeDtypeStruct(shape, kind) for s...]
where the time goes in v7:
time: 37.8 us; the launch traced here: 37.7 us
  Pallas kernels  37 us (98%)
  between operations  0.66 us (2%)
    pallas_call x1, Pallas kernels, on_device(): pl.pallas_call(kernel, out_shape=[jax.ShapeDtypeStruct(shape, kind) for s...  35.4 us
    pallas_call x1, Pallas kernels, on_device(): pl.pallas_call(finish, out_shape=jax.ShapeDtypeStruct(grid.shape, grid.dt...  1.63 us

profile of v7, /device:TPU:0, one launch (start us, length us, event | category | flops | bytes accessed | tf_op | source)
XLA Modules:
  0.0 37.7 jit_solution(2793389532633577526)
XLA Ops:
  0.7 35.4 %shard_map.73 = (bf16[64,2,32,256]{3,2,1,0:T(8,128)(2,1)S(1)}, bf16[32,2,64,128]{3,2,1,0:T(8,128)(2,1)S(1)}, bf16[512,256]{1,0:T(8,128)(2,1)S(1)}, f32[256,256]{1,0:T(8,128)S(1)}) custom-call(bf16[64,2,32,256]{3,2,1,0:T(8,128)(2,1)} %grid_hbm.1, bf16[9,8,64]{2,1,0:T(8,128)(2,1)} %bitcast.3, f32[1,64]{1,0:T(1,128)} %bitcast.5, f32[3,4,64]{2,1,0:T(4,128)} %bitcast.4, ...), custom_call_target="tpu_custom_call" | custom-call | flops 4000000000 | tf_op jit(solution)/shard_map/pallas_call | solution.py:365
  36.0 1.6 %shard_map.74 = bf16[64,2,32,256]{3,2,1,0:T(8,128)(2,1)} custom-call(bf16[64,2,32,256]{3,2,1,0:T(8,128)(2,1)S(1)} %get-tuple-element.9.old_ref, bf16[32,2,64,128]{3,2,1,0:T(8,128)(2,1)S(1)} %get-tuple-element.10.returned, bf16[512,256]{1,0:T(8,128)(2,1)S(1)} %get-tuple-element.11.place, f32[256,256]{1,0:T(8,128)S(1)} %get-tuple-element.12.covered), custom_call_target="tpu_custom_call" | custom-call | tf_op jit(solution)/shard_map/pallas_call | solution.py:405

commit v8 on v7

--- a/solution.py
+++ b/solution.py
@@ -157,7 +157,8 @@
     from_left = jnp.where(tile > 0, edge_in[0], nought[:32, :128])
     from_right = jnp.where(tile < 7, edge_in[1], nought[:32, :128])
 
-    def fix(n, carry):
+    def fix(g, f):
+        n = 2 * g + f
         for i in range(8):
             span = slice(32 * i, 32 * i + 32)
             edge = pltpu.roll(from_left, (128 - 16 * i - n) % 128, 1)
@@ -165,17 +166,16 @@
             span = slice(512 + 32 * i, 544 + 32 * i)
             edge = pltpu.roll(from_right, 127 - 16 * i - n, 1)
             wide[n, span, 128:256] = jnp.where(lane == 127, edge, wide[n, span, 128:256])
-        return carry
-
-    lax.fori_loop(0, 16, fix, 0, unroll=UNROLL)
-
-    def slots(s):
+        return f
+
+
+    def slots(s, frames=(0, 1)):
         lo = 128 * s
 
         @pl.loop(0, 4, unroll=4)
         def _(pair):
             second = half_col[lo : lo + 128] > 0.5
-            for f in range(2):
+            for f in frames:
                 parts = []
                 for e in range(2):
                     g = 2 * pair + e
@@ -216,12 +216,17 @@
     for s in range(2):
         if s == 1:
             fill(1)
-        slots(s)
         if s == 0:
-            pl.semaphore_wait(row_sem, 3)
+            for f in range(2):
+                lax.fori_loop(0, 8, fix, f, unroll=8)
+                slots(0, (f,))
+                if f == 0:
+                    pl.semaphore_wait(row_sem, 3)
+                send(0, lambda to, f=f: outgoing.at[to, f], incoming.at[0, me, f])
         else:
+            slots(1)
             whole(0, outgoing.at[pl.ds(0, 15)]).wait_send()
-        send(s, lambda to, s=s: outgoing.at[16 * s + to], incoming.at[s, me])
+            send(1, lambda to: outgoing.at[16 + to], incoming.at[1, me])
         incoming[s, me] = outgoing[16 * s + me]
 
     offset = (cols((32, 256)) & 31) - rows((32, 256))

time: 37.8 us -> 37.2 us (0.984)
  Pallas kernels: 37 us -> 36.3 us
    pallas_call x1, Pallas kernels: 35.4 us -> 34.6 us  [on_device(): pl.pallas_call(kernel, out_shape=[jax.ShapeDtypeStruct(shape, kind) for s...]
where the time goes in v8:
time: 37.2 us; the launch traced here: 36.9 us
  Pallas kernels  36.3 us (98%)
  between operations  0.66 us (2%)
    pallas_call x1, Pallas kernels, on_device(): pl.pallas_call(kernel, out_shape=[jax.ShapeDtypeStruct(shape, kind) for s...  34.6 us
    pallas_call x1, Pallas kernels, on_device(): pl.pallas_call(finish, out_shape=jax.ShapeDtypeStruct(grid.shape, grid.dt...  1.63 us

profile of v8, /device:TPU:0, one launch (start us, length us, event | category | flops | bytes accessed | tf_op | source)
XLA Modules:
  0.0 36.9 jit_solution(5451602770415672187)
XLA Ops:
  0.7 34.6 %shard_map.73 = (bf16[64,2,32,256]{3,2,1,0:T(8,128)(2,1)S(1)}, bf16[32,2,64,128]{3,2,1,0:T(8,128)(2,1)S(1)}, bf16[512,256]{1,0:T(8,128)(2,1)S(1)}, f32[256,256]{1,0:T(8,128)S(1)}) custom-call(bf16[64,2,32,256]{3,2,1,0:T(8,128)(2,1)} %grid_hbm.1, bf16[9,8,64]{2,1,0:T(8,128)(2,1)} %bitcast.3, f32[1,64]{1,0:T(1,128)} %bitcast.5, f32[3,4,64]{2,1,0:T(4,128)} %bitcast.4, ...), custom_call_target="tpu_custom_call" | custom-call | flops 4000000000 | tf_op jit(solution)/shard_map/pallas_call | solution.py:370
  35.3 1.6 %shard_map.74 = bf16[64,2,32,256]{3,2,1,0:T(8,128)(2,1)} custom-call(bf16[64,2,32,256]{3,2,1,0:T(8,128)(2,1)S(1)} %get-tuple-element.9.old_ref, bf16[32,2,64,128]{3,2,1,0:T(8,128)(2,1)S(1)} %get-tuple-element.10.returned, bf16[512,256]{1,0:T(8,128)(2,1)S(1)} %get-tuple-element.11.place, f32[256,256]{1,0:T(8,128)S(1)} %get-tuple-element.12.covered), custom_call_target="tpu_custom_call" | custom-call | tf_op jit(solution)/shard_map/pallas_call | solution.py:410

commit v9 on v8

--- a/solution.py
+++ b/solution.py
@@ -190,8 +190,8 @@
 
     copies = []
 
-    def send(stage, source, target):
-        for hop in HOPS:
+    def send(stage, source, target, hops=HOPS):
+        for hop in hops:
             to = peer(hop)
             copy = pltpu.make_async_remote_copy(
                 src_ref=source(to),
@@ -222,7 +222,7 @@
                 slots(0, (f,))
                 if f == 0:
                     pl.semaphore_wait(row_sem, 3)
-                send(0, lambda to, f=f: outgoing.at[to, f], incoming.at[0, me, f])
+                send(0, lambda to, f=f: outgoing.at[to, f], incoming.at[0, me, f], HOPS[:: 2 * f - 1])
         else:
             slots(1)
             whole(0, outgoing.at[pl.ds(0, 15)]).wait_send()
@@ -252,7 +252,7 @@
         for s in range(2):
             found = jnp.sum(chosen[:, 128 * s : 128 * s + 128], axis=1, keepdims=True)
             cover = covered if s == 0 else covered_last
-            cover[:, h * 128 : (h + 1) * 128] = jnp.broadcast_to(found, (256, 128))
+            cover[:, h * 128 : (h + 1) * 128] = jnp.broadcast_to(found, (256, 128)).astype(BF16)
 
     for layer in range(4):
         for j in range(3):
@@ -328,9 +328,9 @@
             for h in range(2):
                 span = slice(128 * h, 128 * h + 128)
                 new = value[256 * h : 256 * h + 256, 128 * f : 128 * f + 128]
-                old = old_ref[pl.ds(8 * g, 8), f, :, span].reshape(256, 128).astype(F32)
-                new = jnp.where(covered[:, span] > 0.5, new, old)
-                new_ref[pl.ds(8 * g, 8), f, :, span] = new.reshape(8, 32, 128).astype(BF16)
+                old = old_ref[pl.ds(8 * g, 8), f, :, span].reshape(256, 128)
+                new = jnp.where(covered[:, span] > 0, new.astype(BF16), old)
+                new_ref[pl.ds(8 * g, 8), f, :, span] = new.reshape(8, 32, 128)
 
 
 def finish(old_ref, returned, place, covered, out_hbm, out, sems):
@@ -352,7 +352,7 @@
         ((8, 256, 768), BF16),
         ((8, 256, 768), BF16),
         ((256, 256), BF16),
-        ((256, 256), F32),
+        ((256, 256), BF16),
         ((4, 256, 256), BF16),
         ((12, 64, 128), F32),
         ((64, 256), F32),
@@ -365,7 +365,7 @@
         ((48, 64, 128), F32),
         ((2, 16, 2, 64, 128), BF16),
     ]
-    kinds = [(grid.shape, BF16), ((32, 2, 64, 128), BF16), ((512, 256), BF16), ((256, 256), F32)]
+    kinds = [(grid.shape, BF16), ((32, 2, 64, 128), BF16), ((512, 256), BF16), ((256, 256), BF16)]
     vmem = pl.BlockSpec(memory_space=pltpu.VMEM)
     parts = pl.pallas_call(
         kernel,

time: 37.2 us -> 37.2 us (level)
  no operation moved by 1% of the time
where the time goes in v9:
time: 37.2 us; the launch traced here: 37 us
  Pallas kernels  36.3 us (98%)
  between operations  0.66 us (2%)
    pallas_call x1, Pallas kernels, on_device(): pl.pallas_call(kernel, out_shape=[jax.ShapeDtypeStruct(shape, kind) for s...  34.7 us
    pallas_call x1, Pallas kernels, on_device(): pl.pallas_call(finish, out_shape=jax.ShapeDtypeStruct(grid.shape, grid.dt...  1.63 us

profile of v9, /device:TPU:0, one launch (start us, length us, event | category | flops | bytes accessed | tf_op | source)
XLA Modules:
  0.0 37.0 jit_solution(14093035407885571828)
XLA Ops:
  0.7 34.7 %shard_map.73 = (bf16[64,2,32,256]{3,2,1,0:T(8,128)(2,1)S(1)}, bf16[32,2,64,128]{3,2,1,0:T(8,128)(2,1)S(1)}, bf16[512,256]{1,0:T(8,128)(2,1)S(1)}, bf16[256,256]{1,0:T(8,128)(2,1)S(1)}) custom-call(bf16[64,2,32,256]{3,2,1,0:T(8,128)(2,1)} %grid_hbm.1, bf16[9,8,64]{2,1,0:T(8,128)(2,1)} %bitcast.3, f32[1,64]{1,0:T(1,128)} %bitcast.5, f32[3,4,64]{2,1,0:T(4,128)} %bitcast.4, ...), custom_call_target="tpu_custom_call" | custom-call | flops 4000000000 | tf_op jit(solution)/shard_map/pallas_call | solution.py:370
  35.4 1.6 %shard_map.74 = bf16[64,2,32,256]{3,2,1,0:T(8,128)(2,1)} custom-call(bf16[64,2,32,256]{3,2,1,0:T(8,128)(2,1)S(1)} %get-tuple-element.9.old_ref, bf16[32,2,64,128]{3,2,1,0:T(8,128)(2,1)S(1)} %get-tuple-element.10.returned, bf16[512,256]{1,0:T(8,128)(2,1)S(1)} %get-tuple-element.11.place, bf16[256,256]{1,0:T(8,128)(2,1)S(1)} %get-tuple-element.12.covered), custom_call_target="tpu_custom_call" | custom-call | tf_op jit(solution)/shard_map/pallas_call | solution.py:410
